TPU v7x, 256 devices: a whole 4x4x8 slice. The times are simulated.
256 devices in a mesh: group: 8 (over z), shard: 32 (over x, y, core).
Axes of the slice: x: 4, y: 4, z: 8, core: 2. Of those that a mesh axis runs over, the one named last changes fastest.
Arguments:
- offer_attribute_matrix: bfloat16 [1024, 128, 1024], P(('group', 'shard')), may hold values from -6 to 6
- kept_offers: int32 [1024, 32], P(('group', 'shard')), may hold values from 0 to 127, as said below
- expert_target: int32 [1024, 6], P(('group', 'shard')), may hold values from 0 to 31, all different within a row; in each aligned block of 4 rows (0 to 3, 4 to 7, ...) at most 2 rows name the same one
- sequence_extent: int32 [1024], P(('group', 'shard')), may hold values from 1 to 128
- behaviour_sequence: bfloat16 [1024, 128, 512], P(('group', 'shard')), may hold values from -6 to 6
- inner_projection_matrix: bfloat16 [1024, 1024], replicated, may hold values from -0.1875 to 0.1875
- student_rating_vector: bfloat16 [1024], replicated, may hold values from -0.1875 to 0.1875
- asking_matrix: bfloat16 [32, 1024, 512], P('shard'), may hold values from -0.1875 to 0.1875
- lookup_matrix: bfloat16 [32, 512, 512], P('shard'), may hold values from -0.25 to 0.25
- content_matrix: bfloat16 [32, 512, 512], P('shard'), may hold values from -0.25 to 0.25
- expert_rating_vector: bfloat16 [32, 512], P('shard'), may hold values from -1.1953125 to 1.1953125
Outputs:
- grad_hidden: float32 [1024, 1024], P('shard')
- grad_score: float32 [1024], replicated
Inputs may be any that keep to these rules, and one draw needn't show every extreme that they name: `kept_offers`: the 32 survivors of a request are distinct candidates. `expert_target`: each request names 6 distinct experts; the requests of one device name any expert at most 2 times, a bound that some block reaches.
All inputs are finite; a program needn't handle non-finite values.
Results may differ from a plain program's by a relative error of at most 0.005.
Values may be sent and summed in bfloat16 or wider, within the bound.
A program may use at most 128 MiB of HBM per device.

v0:
```python
import functools

import jax
import jax.numpy as jnp
from jax import lax
from jax.sharding import Mesh
from jax.sharding import PartitionSpec as P

ATTENDER_GANGS = 8
SHARD = ("shard_0", "shard_1", "shard_2")
GROUP_SHARD = ("group", "shard_0", "shard_1", "shard_2")


def in_blocks(value, dim, devices):
    before, after = (value.shape[:dim], value.shape[dim + 1 :])
    return jnp.moveaxis(value.reshape(*before, devices, -1, *after), dim, 0)


def laid_out(blocks, dim):
    blocks = jnp.moveaxis(blocks, 0, dim)
    lengths = blocks.shape
    return blocks.reshape(*lengths[:dim], lengths[dim] * lengths[dim + 1], *lengths[dim + 2 :])


def turned_blocks(blocks, axes, order):
    inside = blocks.shape[1:]
    result = blocks.reshape(*(lax.axis_size(a) for a in axes), *inside)
    for k in order:
        result = lax.all_to_all(result, axes[k], k, k, tiled=True)
    return result.reshape(-1, *inside)


def core_and_chips(value, groups, order, split_dim, concat_dim):
    devices = lax.axis_size(groups[0]) * lax.axis_size(groups[1])
    blocks = in_blocks(value, split_dim, devices)
    return laid_out(turned_blocks(blocks, groups, order), concat_dim)


def sum_at_owner(value, axis, dim):
    blocks = in_blocks(value, dim, lax.axis_size(axis))
    arrived = lax.all_to_all(blocks, axis, split_axis=0, concat_axis=0, tiled=True)
    return arrived.sum(axis=0)


def from_everyone(value, axis):
    copies = jnp.broadcast_to(value, (lax.axis_size(axis), *value.shape))
    return lax.all_to_all(copies, axis, split_axis=0, concat_axis=0, tiled=True)


def over_copies(value, axis):
    everything = from_everyone(value, axis)
    return jnp.sum(everything, axis=0)


def one_axis_at_a_time(value, axes):
    return functools.reduce(lax.psum, axes, value)


def body(
    offer_attribute_matrix,
    kept_offers,
    expert_target,
    sequence_extent,
    behaviour_sequence,
    inner_projection_matrix,
    student_rating_vector,
    asking_matrix,
    lookup_matrix,
    content_matrix,
    expert_rating_vector,
):
    requests_here, offer_number, attribute_span = offer_attribute_matrix.shape
    kept_number = kept_offers.shape[1]
    hist_slots, focus_span = (behaviour_sequence.shape[1], behaviour_sequence.shape[2])
    rankers_each = expert_target.shape[1]
    ranker_count = lax.axis_size(SHARD)
    routed_rows = requests_here * rankers_each
    capacity = max(2, (routed_rows + ranker_count - 1) // ranker_count + 1)
    place_number = ranker_count * capacity
    row_dest = expert_target.reshape(routed_rows)
    by_expert = (row_dest[:, None] == jnp.arange(ranker_count, dtype=jnp.int32)[None, :]).astype(
        jnp.int32
    )
    earlier = jnp.cumsum(by_expert, axis=0) - by_expert
    rank_in = jnp.sum(earlier * by_expert, axis=1)
    slot_of = row_dest * capacity + rank_in
    placing = slot_of[:, None] == jnp.arange(place_number, dtype=jnp.int32)[None, :]
    placing = placing.reshape(requests_here, rankers_each, place_number)
    placing_b = placing.astype(jnp.bfloat16)
    placing_f = placing.astype(jnp.float32)
    chosen_lines = (
        kept_offers[:, :, None] == jnp.arange(offer_number, dtype=jnp.int32)[None, None, :]
    ).astype(jnp.bfloat16)
    chosen = jnp.einsum(
        "rkc,rcf->rkf", chosen_lines, offer_attribute_matrix, preferred_element_type=jnp.float32
    ).astype(jnp.bfloat16)
    send_rows = jnp.einsum(
        "rts,rkf->skf", placing_b, chosen, preferred_element_type=jnp.float32
    ).astype(jnp.bfloat16)
    send_hist = jnp.einsum(
        "rts,rjf->sjf", placing_b, behaviour_sequence, preferred_element_type=jnp.float32
    ).astype(jnp.bfloat16)
    send_len = jnp.einsum("rts,r->s", placing_f, sequence_extent.astype(jnp.float32)).astype(
        jnp.bfloat16
    )
    arriving_lines, recv_hist, recv_len = (
        lax.all_to_all(send_rows, SHARD, split_axis=0, concat_axis=0, tiled=True),
        lax.all_to_all(send_hist, SHARD, split_axis=0, concat_axis=0, tiled=True),
        lax.all_to_all(send_len, SHARD, split_axis=0, concat_axis=0, tiled=True),
    )
    single_attender_span = focus_span // ATTENDER_GANGS
    segment_places = 16
    segment_number = place_number // segment_places

    def ranker_block(block):
        rows, hist_rows, lens = block
        queries = jnp.dot(
            rows.reshape(-1, attribute_span), asking_matrix[0], preferred_element_type=jnp.float32
        )
        queries = queries.astype(jnp.bfloat16).reshape(
            segment_places, kept_number, ATTENDER_GANGS, single_attender_span
        )
        flat_hist = hist_rows.reshape(-1, focus_span)
        key_rows = jnp.dot(flat_hist, lookup_matrix[0], preferred_element_type=jnp.float32)
        key_rows = key_rows.astype(jnp.bfloat16).reshape(
            segment_places, hist_slots, ATTENDER_GANGS, single_attender_span
        )
        value_rows = jnp.dot(flat_hist, content_matrix[0], preferred_element_type=jnp.float32)
        value_rows = value_rows.astype(jnp.bfloat16).reshape(
            segment_places, hist_slots, ATTENDER_GANGS, single_attender_span
        )
        logits = jnp.einsum(
            "skhd,sjhd->shkj", queries, key_rows, preferred_element_type=jnp.float32
        ) * single_attender_span ** (-0.5)
        lengths = jnp.maximum(lens.astype(jnp.float32), jnp.float32(1.0))
        visible = (
            jnp.arange(hist_slots, dtype=jnp.float32)[None, None, None, :]
            < lengths[:, None, None, None]
        )
        weights = jnp.where(visible, jnp.exp(logits), jnp.float32(0.0))
        attn_probs = (weights / jnp.sum(weights, axis=-1, keepdims=True)).astype(jnp.bfloat16)
        mixed_context = jnp.einsum(
            "shkj,sjhd->skhd", attn_probs, value_rows, preferred_element_type=jnp.float32
        )
        mixed_context = mixed_context.reshape(segment_places, kept_number, focus_span)
        return jnp.sum(mixed_context * expert_rating_vector[0].astype(jnp.float32), axis=-1)

    mentor_output = lax.map(
        ranker_block,
        (
            arriving_lines.reshape(segment_number, segment_places, kept_number, attribute_span),
            recv_hist.reshape(segment_number, segment_places, hist_slots, focus_span),
            recv_len.reshape(segment_number, segment_places),
        ),
    )
    mentor_output = mentor_output.reshape(place_number, kept_number)
    returned = core_and_chips(mentor_output, (("shard_0", "shard_1"), "shard_2"), (1, 0), 0, 0)
    own_teacher = (
        jnp.einsum("rts,sk->rk", placing_f, returned, precision=lax.Precision.HIGHEST)
        / rankers_each
    )
    score_vec = student_rating_vector.astype(jnp.float32)
    flat_feats = offer_attribute_matrix.reshape(requests_here * offer_number, attribute_span)
    preact = jnp.dot(flat_feats, inner_projection_matrix, preferred_element_type=jnp.float32)
    hidden = jnp.maximum(preact, jnp.float32(0.0))
    scores = jnp.sum(hidden * score_vec, axis=-1).reshape(requests_here, offer_number)
    exp_scores = jnp.exp(scores)
    student = exp_scores / jnp.sum(exp_scores, axis=-1, keepdims=True)
    exp_teacher = jnp.exp(own_teacher)
    target = exp_teacher / jnp.sum(exp_teacher, axis=-1, keepdims=True)
    target_cand = jnp.sum(target[:, :, None] * chosen_lines.astype(jnp.float32), axis=1)
    score_grad = (student - target_cand).reshape(requests_here * offer_number, 1)
    hidden_grad = (score_grad * score_vec * (preact > 0).astype(jnp.float32)).astype(jnp.bfloat16)
    local_score = jnp.sum(score_grad * hidden, axis=0)
    grad_rows = sum_at_owner(
        lax.dot_general(
            flat_feats, hidden_grad, (((0,), (0,)), ((), ())), preferred_element_type=jnp.float32
        ),
        SHARD,
        0,
    )
    grad_hidden = over_copies(grad_rows, "group")
    grad_score = one_axis_at_a_time(local_score, GROUP_SHARD)
    return (grad_hidden, grad_score)


def solution(mesh):
    torus = Mesh(
        mesh.devices.reshape(mesh.shape["group"], 4, 4, 2),
        ("group", "shard_0", "shard_1", "shard_2"),
    )
    return jax.shard_map(
        body,
        mesh=torus,
        in_specs=(
            P(GROUP_SHARD, None, None),
            P(GROUP_SHARD, None),
            P(GROUP_SHARD, None),
            P(GROUP_SHARD),
            P(GROUP_SHARD, None, None),
            P(),
            P(),
            P(SHARD, None, None),
            P(SHARD, None, None),
            P(SHARD, None, None),
            P(SHARD, None),
        ),
        out_specs=(P(SHARD, None), P()),
        check_vma=False,
    )
```

profile of v0, /device:TPU:2, one launch (start us, length us, event | category | flops | bytes accessed | tf_op | source)
XLA Modules:
  0.0 461.9 jit_solution(16846945645825278984)
XLA Ops:
  4.3 7.6 %all-to-all-start.1 = ((bf16[32,2,1]{1,2,0:T(2,128)(2,1)}), bf16[32,2,1]{1,2,0:T(2,128)(2,1)S(1)}, u32[]{:S(2)}, u32[]{:S(2)}) async-start(bf16[32,2,1]{1,2,0:T(2,128)(2,1)} %all_to_all.32), calls=%async_computation.1 | async-start | bytes 32768 | tf_op jit(solution)/shard_map/all_to_all | solution.py:109
  14.8 4.3 copy.71
  19.1 7.6 %all-to-all-start.2 = ((bf16[64,32,1024]{2,1,0:T(8,128)(2,1)}), bf16[64,32,1024]{2,1,0:T(8,128)(2,1)}, u32[]{:S(2)}, u32[]{:S(2)}) async-start(bf16[64,32,1024]{2,1,0:T(8,128)(2,1)} %copy.71), calls=%async_computation.2 | async-start | bytes 8388608 | tf_op jit(solution)/shard_map/all_to_all | solution.py:107
  26.7 5.6 %convolution_convert_fusion.3 = bf16[64,128,512]{2,0,1:T(8,128)(2,1)} fusion(bf16[4,128,512]{2,1,0:T(8,128)(2,1)S(1)} %copy-done.5, bf16[4,64]{1,0:T(4,128)(2,1)S(1)} %get-tuple-element.68), kind=kOutput, calls=%fused_computation.30 | convolution fusion | flops 33554432 | bytes 8913408 | tf_op jit(solution)/shard_map/rts,rjf->sjf/dot_general | solution.py:100
  32.3 11.3 %copy.68 = bf16[64,128,512]{2,1,0:T(8,128)(2,1)} copy(bf16[64,128,512]{2,0,1:T(8,128)(2,1)} %convolution_convert_fusion.3) | data formatting | bytes 16777216 | tf_op jit(solution)/shard_map/convert_element_type | solution.py:102
  43.7 33.2 %all-to-all-done.2 = bf16[64,32,1024]{2,1,0:T(8,128)(2,1)} async-done(((bf16[64,32,1024]{2,1,0:T(8,128)(2,1)}), bf16[64,32,1024]{2,1,0:T(8,128)(2,1)}, u32[]{:S(2)}, u32[]{:S(2)}) %all-to-all-start.2) | async-done | bytes 4194336 | tf_op jit(solution)/shard_map/all_to_all | solution.py:107
  76.8 9.3 %all-to-all-start = ((bf16[64,128,512]{2,1,0:T(8,128)(2,1)}), bf16[64,128,512]{2,1,0:T(8,128)(2,1)}, u32[]{:S(2)}, u32[]{:S(2)}) async-start(bf16[64,128,512]{2,1,0:T(8,128)(2,1)} %copy.68), calls=%async_computation | async-start | bytes 16777216 | tf_op jit(solution)/shard_map/all_to_all | solution.py:108
  88.9 102.0 %all-to-all-done = bf16[64,128,512]{2,1,0:T(8,128)(2,1)} async-done(((bf16[64,128,512]{2,1,0:T(8,128)(2,1)}), bf16[64,128,512]{2,1,0:T(8,128)(2,1)}, u32[]{:S(2)}, u32[]{:S(2)}) %all-to-all-start) | async-done | bytes 8388640 | tf_op jit(solution)/shard_map/all_to_all | solution.py:108
  190.9 105.1 %while.10 = (s32[]{:T(128)}, f32[4,16,32]{2,1,0:T(8,128)S(1)}, bf16[4,16,128,512]{3,2,1,0:T(8,128)(2,1)}, bf16[1,512,512]{2,1,0:T(8,128)(2,1)}, bf16[4,16]{1,0:T...) while((s32[]{:T(128)}, f32[4,16,32]{2,1,0:T(8,128)S(1)}, ...), condition=%wide.region_9.10_spmd, body=%wide.region_6.9_spmd.sunk | while | flops 2825123840 | bytes 61932960 | solution.py:148
  195.4 3.7 reshape.151
  201.9 6.0 %fusion.65 = (f32[16,8,32]{2,1,0:T(8,128)S(1)}, f32[16,8,32,128]{3,2,1,0:T(8,128)}) fusion(pred[16,128]{1,0:T(8,128)(4,1)S(1)} %iota_compare_fusion.6, bf16[16,128,8,64]{3,2,1,0:T(8,128)(2,1)} %reshape.151, bf16[16,32,8,64]{3,2,1,0:T(8,128)(2,1)S(1)} %reshape.152), kind=kOutput, calls=%fused_computation.9.clone.1 | convolution fusion | flops 68677632 | bytes 4737024 | tf_op jit(solution)/shard_map/while/body/eval_jaxpr/skhd,sjhd->shkj/dot_general | solution.py:132
  209.2 3.7 reshape.150
  212.9 4.2 multiply_reduce_fusion.5
  221.6 3.7 reshape.151
  228.2 6.0 %fusion.65 = (f32[16,8,32]{2,1,0:T(8,128)S(1)}, f32[16,8,32,128]{3,2,1,0:T(8,128)}) fusion(pred[16,128]{1,0:T(8,128)(4,1)S(1)} %iota_compare_fusion.6, bf16[16,128,8,64]{3,2,1,0:T(8,128)(2,1)} %reshape.151, bf16[16,32,8,64]{3,2,1,0:T(8,128)(2,1)S(1)} %reshape.152), kind=kOutput, calls=%fused_computation.9.clone.1 | convolution fusion | flops 68677632 | bytes 4737024 | tf_op jit(solution)/shard_map/while/body/eval_jaxpr/skhd,sjhd->shkj/dot_general | solution.py:132
  235.4 3.7 reshape.150
  239.2 4.2 multiply_reduce_fusion.5
  247.9 3.7 reshape.151
  254.5 6.0 %fusion.65 = (f32[16,8,32]{2,1,0:T(8,128)S(1)}, f32[16,8,32,128]{3,2,1,0:T(8,128)}) fusion(pred[16,128]{1,0:T(8,128)(4,1)S(1)} %iota_compare_fusion.6, bf16[16,128,8,64]{3,2,1,0:T(8,128)(2,1)} %reshape.151, bf16[16,32,8,64]{3,2,1,0:T(8,128)(2,1)S(1)} %reshape.152), kind=kOutput, calls=%fused_computation.9.clone.1 | convolution fusion | flops 68677632 | bytes 4737024 | tf_op jit(solution)/shard_map/while/body/eval_jaxpr/skhd,sjhd->shkj/dot_general | solution.py:132
  261.7 3.7 reshape.150
  265.5 4.2 multiply_reduce_fusion.5
  274.2 3.7 reshape.151
  280.8 6.0 %fusion.65 = (f32[16,8,32]{2,1,0:T(8,128)S(1)}, f32[16,8,32,128]{3,2,1,0:T(8,128)}) fusion(pred[16,128]{1,0:T(8,128)(4,1)S(1)} %iota_compare_fusion.6, bf16[16,128,8,64]{3,2,1,0:T(8,128)(2,1)} %reshape.151, bf16[16,32,8,64]{3,2,1,0:T(8,128)(2,1)S(1)} %reshape.152), kind=kOutput, calls=%fused_computation.9.clone.1 | convolution fusion | flops 68677632 | bytes 4737024 | tf_op jit(solution)/shard_map/while/body/eval_jaxpr/skhd,sjhd->shkj/dot_general | solution.py:132
  291.8 4.2 multiply_reduce_fusion.5
  296.2 3.7 all_to_all.40
  301.9 25.2 %all-to-all-start.4 = ((f32[16,1,128]{2,1,0:T(1,128)}), f32[16,1,128]{2,1,0:T(1,128)S(1)}, u32[]{:S(2)}, u32[]{:S(2)}) async-start(f32[16,1,128]{2,1,0:T(1,128)} %reshape.144), calls=%async_computation.4 | async-start | bytes 16384 | tf_op jit(solution)/shard_map/all_to_all | solution.py:29
  327.1 6.0 %all-to-all-done.4 = f32[16,1,128]{2,1,0:T(1,128)S(1)} async-done(((f32[16,1,128]{2,1,0:T(1,128)}), f32[16,1,128]{2,1,0:T(1,128)S(1)}, u32[]{:S(2)}, u32[]{:S(2)}) %all-to-all-start.4) | async-done | bytes 8224 | tf_op jit(solution)/shard_map/all_to_all | solution.py:29
  337.5 53.1 %all_to_all.41 = f32[32,32,1024]{2,1,0:T(8,128)} all-to-all(f32[32,32,1024]{2,1,0:T(8,128)S(1)} %bitcast.80), channel_id=1, replica_groups=mesh['group'=8,'shard_0'=4,'shard_1'=4,'shard_2'=2] {'shard_0','shard_1'..., dimensions={0} | all-to-all | bytes 8388608 | tf_op jit(solution)/shard_map/all_to_all | solution.py:41
  394.1 8.5 %all-to-all-start.6 = ((f32[8,32,1024]{2,1,0:T(8,128)}), f32[8,32,1024]{2,1,0:T(8,128)S(1)}, u32[]{:S(2)}, u32[]{:S(2)}) async-start(f32[8,32,1024]{2,1,0:T(8,128)} %broadcast_in_dim.25), calls=%async_computation.6 | async-start | bytes 2097152 | tf_op jit(solution)/shard_map/all_to_all | solution.py:47
  404.6 34.6 %psum.28 = f32[1024]{0:T(1024)S(1)} all-reduce(f32[1024]{0:T(1024)S(1)} %multiply_reduce_fusion.1), channel_id=1, replica_groups=mesh['group'=8,'shard_0'=4,'shard_1'=4,'shard_2'=2] {'group'}, use_global_device_ids=true, to_apply=%region_15.16 | all-reduce | flops 1024 | bytes 8192 | tf_op jit(solution)/shard_map/psum | solution.py:56
  439.1 9.7 %psum.29 = f32[1024]{0:T(1024)S(1)} all-reduce(f32[1024]{0:T(1024)S(1)} %psum.28), channel_id=1, replica_groups=mesh['group'=8,'shard_0'=4,'shard_1'=4,'shard_2'=2] {'shard_0'}, use_global_device_ids=true, to_apply=%region_16.17 | all-reduce | flops 1024 | bytes 8192 | tf_op jit(solution)/shard_map/psum | solution.py:56
  448.9 9.2 %psum.30 = f32[1024]{0:T(1024)S(1)} all-reduce(f32[1024]{0:T(1024)S(1)} %psum.29), channel_id=1, replica_groups=mesh['group'=8,'shard_0'=4,'shard_1'=4,'shard_2'=2] {'shard_1'}, use_global_device_ids=true, to_apply=%region_17.18 | all-reduce | flops 1024 | bytes 8192 | tf_op jit(solution)/shard_map/psum | solution.py:56
  (138 shorter events, 63.6 us)
Async XLA Ops:
  0.6 85.5 %copy-start = (bf16[1024,1024]{1,0:T(8,128)(2,1)S(1)}, bf16[1024,1024]{1,0:T(8,128)(2,1)}, u32[]{:S(2)}) copy-start(bf16[1024,1024]{1,0:T(8,128)(2,1)} %param.18) | copy-start | bytes 6291460
  4.3 14.8 %all-to-all-start.1 = ((bf16[32,2,1]{1,2,0:T(2,128)(2,1)}), bf16[32,2,1]{1,2,0:T(2,128)(2,1)S(1)}, u32[]{:S(2)}, u32[]{:S(2)}) async-start(bf16[32,2,1]{1,2,0:T(2,128)(2,1)} %all_to_all.32), calls=%async_computation.1 | async-start | bytes 32768 | tf_op jit(solution)/shard_map/all_to_all | solution.py:109
  19.1 7.6 %copy-start.5 = (bf16[4,128,512]{2,1,0:T(8,128)(2,1)S(1)}, bf16[4,128,512]{2,1,0:T(8,128)(2,1)}, u32[]{:S(2)}) copy-start(bf16[4,128,512]{2,1,0:T(8,128)(2,1)} %param.17) | copy-start | bytes 1572868
  19.1 57.7 %all-to-all-start.2 = ((bf16[64,32,1024]{2,1,0:T(8,128)(2,1)}), bf16[64,32,1024]{2,1,0:T(8,128)(2,1)}, u32[]{:S(2)}, u32[]{:S(2)}) async-start(bf16[64,32,1024]{2,1,0:T(8,128)(2,1)} %copy.71), calls=%async_computation.2 | async-start | bytes 8388608 | tf_op jit(solution)/shard_map/all_to_all | solution.py:107
  43.7 42.5 %copy-start.8 = (bf16[1024]{0:T(1024)(128)(2,1)S(1)}, bf16[1024]{0:T(1024)(128)(2,1)}, u32[]{:S(2)}) copy-start(bf16[1024]{0:T(1024)(128)(2,1)} %param.19) | copy-start | bytes 6148
  43.7 42.5 %copy-start.4 = (bf16[4,128,1024]{2,1,0:T(8,128)(2,1)S(1)}, bf16[4,128,1024]{2,1,0:T(8,128)(2,1)}, u32[]{:S(2)}) copy-start(bf16[4,128,1024]{2,1,0:T(8,128)(2,1)} %param.13) | copy-start | bytes 3145732
  76.8 114.0 %all-to-all-start = ((bf16[64,128,512]{2,1,0:T(8,128)(2,1)}), bf16[64,128,512]{2,1,0:T(8,128)(2,1)}, u32[]{:S(2)}, u32[]{:S(2)}) async-start(bf16[64,128,512]{2,1,0:T(8,128)(2,1)} %copy.68), calls=%async_computation | async-start | bytes 16777216 | tf_op jit(solution)/shard_map/all_to_all | solution.py:108
  86.2 104.7 %copy-start.6 = (bf16[1,512]{1,0:T(2,128)(2,1)S(1)}, bf16[1,512]{1,0:T(2,128)(2,1)}, u32[]{:S(2)}) copy-start(bf16[1,512]{1,0:T(2,128)(2,1)} %param.23) | copy-start | bytes 3076
  190.9 143.4 %copy-start.7 = (s32[4,32]{1,0:T(4,128)S(1)}, s32[4,32]{1,0:T(4,128)}, u32[]{:S(2)}) copy-start(s32[4,32]{1,0:T(4,128)} %param.14) | copy-start | bytes 1540
  190.9 3.2 copy-start.11
  192.7 1.4 copy-start.2
  199.0 1.5 copy-start.9
  201.9 6.0 %copy-start.3 = (bf16[1,16,128,512]{3,2,1,0:T(8,128)(2,1)S(1)}, bf16[1,16,128,512]{3,2,1,0:T(8,128)(2,1)}, u32[]{:S(2)}) copy-start(bf16[1,16,128,512]{3,2,1,0:T(8,128)(2,1)} %copy-done.2) | copy-start | bytes 6291460 | tf_op jit(solution)/shard_map/while
  201.9 6.0 %copy-start.10 = (bf16[1,512,512]{2,1,0:T(8,128)(2,1)S(1)}, bf16[1,512,512]{2,1,0:T(8,128)(2,1)}, u32[]{:S(2)}) copy-start(bf16[1,512,512]{2,1,0:T(8,128)(2,1)} %get-tuple-element.176) | copy-start | bytes 1572868 | tf_op jit(solution)/shard_map/while
  217.2 3.2 copy-start.11
  219.0 1.4 copy-start.2
  225.3 1.5 copy-start.9
  228.2 6.0 %copy-start.3 = (bf16[1,16,128,512]{3,2,1,0:T(8,128)(2,1)S(1)}, bf16[1,16,128,512]{3,2,1,0:T(8,128)(2,1)}, u32[]{:S(2)}) copy-start(bf16[1,16,128,512]{3,2,1,0:T(8,128)(2,1)} %copy-done.2) | copy-start | bytes 6291460 | tf_op jit(solution)/shard_map/while
  228.2 6.0 %copy-start.10 = (bf16[1,512,512]{2,1,0:T(8,128)(2,1)S(1)}, bf16[1,512,512]{2,1,0:T(8,128)(2,1)}, u32[]{:S(2)}) copy-start(bf16[1,512,512]{2,1,0:T(8,128)(2,1)} %get-tuple-element.176) | copy-start | bytes 1572868 | tf_op jit(solution)/shard_map/while
  243.4 3.2 copy-start.11
  245.3 1.4 copy-start.2
  251.6 1.5 copy-start.9
  254.5 6.0 %copy-start.3 = (bf16[1,16,128,512]{3,2,1,0:T(8,128)(2,1)S(1)}, bf16[1,16,128,512]{3,2,1,0:T(8,128)(2,1)}, u32[]{:S(2)}) copy-start(bf16[1,16,128,512]{3,2,1,0:T(8,128)(2,1)} %copy-done.2) | copy-start | bytes 6291460 | tf_op jit(solution)/shard_map/while
  254.5 6.0 %copy-start.10 = (bf16[1,512,512]{2,1,0:T(8,128)(2,1)S(1)}, bf16[1,512,512]{2,1,0:T(8,128)(2,1)}, u32[]{:S(2)}) copy-start(bf16[1,512,512]{2,1,0:T(8,128)(2,1)} %get-tuple-element.176) | copy-start | bytes 1572868 | tf_op jit(solution)/shard_map/while
  269.7 3.2 copy-start.11
  271.6 1.4 copy-start.2
  277.9 1.5 copy-start.9
  280.8 6.0 %copy-start.3 = (bf16[1,16,128,512]{3,2,1,0:T(8,128)(2,1)S(1)}, bf16[1,16,128,512]{3,2,1,0:T(8,128)(2,1)}, u32[]{:S(2)}) copy-start(bf16[1,16,128,512]{3,2,1,0:T(8,128)(2,1)} %copy-done.2) | copy-start | bytes 6291460 | tf_op jit(solution)/shard_map/while
  280.8 6.0 %copy-start.10 = (bf16[1,512,512]{2,1,0:T(8,128)(2,1)S(1)}, bf16[1,512,512]{2,1,0:T(8,128)(2,1)}, u32[]{:S(2)}) copy-start(bf16[1,512,512]{2,1,0:T(8,128)(2,1)} %get-tuple-element.176) | copy-start | bytes 1572868 | tf_op jit(solution)/shard_map/while
  301.9 31.3 %all-to-all-start.4 = ((f32[16,1,128]{2,1,0:T(1,128)}), f32[16,1,128]{2,1,0:T(1,128)S(1)}, u32[]{:S(2)}, u32[]{:S(2)}) async-start(f32[16,1,128]{2,1,0:T(1,128)} %reshape.144), calls=%async_computation.4 | async-start | bytes 16384 | tf_op jit(solution)/shard_map/all_to_all | solution.py:29
  394.1 67.0 %all-to-all-start.6 = ((f32[8,32,1024]{2,1,0:T(8,128)}), f32[8,32,1024]{2,1,0:T(8,128)S(1)}, u32[]{:S(2)}, u32[]{:S(2)}) async-start(f32[8,32,1024]{2,1,0:T(8,128)} %broadcast_in_dim.25), calls=%async_computation.6 | async-start | bytes 2097152 | tf_op jit(solution)/shard_map/all_to_all | solution.py:47
  402.6 59.3 %copy-start.1 = (bf16[1024,1024]{1,0:T(8,128)(2,1)S(1)}, bf16[1024,1024]{1,0:T(8,128)(2,1)}, u32[]{:S(2)}) copy-start(bf16[1024,1024]{1,0:T(8,128)(2,1)} %param.18) | copy-start | bytes 6291460
where the time goes:
time: 465 us; the launch traced here: 462 us
  waiting for transfers between devices  141 us (30%)
  blocking collectives  113 us (24%)
  local copies, waits for them, and re-layouts  71.1 us (15%)
  matrix products  68.6 us (15%)
  starting transfers between devices  58.1 us (12%)
  other arithmetic  8.46 us (2%)
    all_to_all x1, waiting for transfers between devices, body(): lax.all_to_all(send_hist, SHARD, split_axis=0, concat_axis=0, tiled=True)  102 us
    psum x4, blocking collectives, one_axis_at_a_time(): return functools.reduce(lax.psum, axes, value)  56.5 us
    all_to_all x1, blocking collectives, sum_at_owner(): lax.all_to_all(blocks, axis, split_axis=0, concat_axis=0, tiled=True)  53.1 us
    all_to_all x1, waiting for transfers between devices, body(): lax.all_to_all(send_rows, SHARD, split_axis=0, concat_axis=0, tiled=True)  33.2 us
    all_to_all x1, starting transfers between devices, turned_blocks(): result = lax.all_to_all(result, axes[k], k, k, tiled=True)  25.2 us
    dot_general x4, matrix products, ranker_block(): jnp.einsum('skhd,sjhd->shkj', queries, key_rows, preferred_element_type=j...  23.8 us
    dot_general x4, matrix products, ranker_block(): jnp.einsum('shkj,sjhd->skhd', attn_probs, value_rows, preferred_element_t...  16.8 us
    reshape x4, local copies, waits for them, and re-layouts, ranker_block(): key_rows.astype(jnp.bfloat16)  14.7 us
  transfers between devices with their start and end apart: 5, of which 3 were waited for; matrix products, arithmetic and copies ran while one was open for 6% of the time, Pallas kernels for 0%

commit v1 on v0

v1 whole, which is shorter than its diff:
```python
import functools

import jax
import jax.numpy as jnp
from jax import lax
from jax.experimental import pallas as pl
from jax.experimental.pallas import tpu as pltpu
from jax.sharding import Mesh
from jax.sharding import PartitionSpec as P

MESH = pl.DeviceIdType.MESH
F32 = jnp.float32
BF16 = jnp.bfloat16
HEADS = 8
GZ, GX, GY, GC = "group", "shard_0", "shard_1", "shard_2"
SHARD = (GX, GY, GC)
GROUP_SHARD = (GZ, GX, GY, GC)
NX, NY, NZ = 4, 4, 8
SLICE = 96
SPLIT = SLICE * NZ
NT = (((1,), (1,)), ((), ()))
TN = (((0,), (0,)), ((), ()))


def dot(a, b, dims=(((1,), (0,)), ((), ()))):
    return lax.dot_general(a, b, dims, preferred_element_type=F32)


def at(axis, step, size):
    return {axis: lax.rem(lax.axis_index(axis) + (step % size), size)}


def gather_kernel(
    x_ref, kept_ref, w1_ref, v_ref, hist_ref, wq_ref, wk_ref, wv_ref, rat_ref, meta_ref,
    sel_all, hist_all, meta_all, wq_all, wk_all, wr_all, hid_out, st_out, xt_out,
    x_v, w1_v, wv_v, sel_v, wr_v, hid_v, st_v, xt_v, send_sem, recv_sem, load_sem,
):
    z = lax.axis_index(GZ)
    other = {GC: 1 - lax.axis_index(GC)}
    right = {a: at(a, 1, n) for a, n in ((GX, NX), (GY, NY), (GZ, NZ))}
    left = {a: at(a, -1, n) for a, n in ((GX, NX), (GY, NY), (GZ, NZ))}
    used = []

    def send(src, dst, device):
        k = len(used)
        copy = pltpu.make_async_remote_copy(
            src_ref=src, dst_ref=dst, send_sem=send_sem.at[k], recv_sem=recv_sem.at[k],
            device_id=device, device_id_type=MESH,
        )
        copy.start()
        used.append(copy)
        return copy

    local = []

    def load(src, dst):
        copy = pltpu.make_async_copy(src, dst, load_sem.at[len(local)])
        copy.start()
        local.append(copy)
        return copy

    load_x = load(x_ref, x_v)
    load_wv = load(wv_ref, wv_v)
    load_w1 = load(w1_ref, w1_v)

    barrier = pltpu.get_barrier_semaphore()
    peers = [*right.values(), *left.values(), other]
    for peer in peers:
        pl.semaphore_signal(barrier, inc=1, device_id=peer, device_id_type=MESH)
    pl.semaphore_wait(barrier, len(peers))

    def zrows(step, start=0, size=SLICE):
        plane = lax.rem(z + (step % NZ), NZ)
        return pl.ds(pl.multiple_of(plane * SLICE + start, 16), size)

    half = SLICE // 2
    tail = (1024 - SPLIT) // 2
    yR, yL, xR, xL, zR, zL = right[GY], left[GY], right[GX], left[GX], right[GZ], left[GZ]

    zsR = send(wq_ref.at[zrows(0)], wq_all.at[1, zrows(0)], yR)
    zsL = send(wq_ref.at[zrows(0)], wq_all.at[0, zrows(0)], yL)

    def x_hist(h, device, slot):
        return send(hist_ref.at[pl.ds(2 * h, 2)], hist_all.at[slot, 0, pl.ds(2 * h, 2)], device)

    def x_sel(h, device, slot):
        return send(sel_v.at[pl.ds(2 * h, 2)], sel_all.at[slot, 0, pl.ds(2 * h, 2)], device)

    def y_k(h, device, slot):
        rows = pl.ds(256 * h, 256)
        return send(wk_ref.at[rows], wk_all.at[slot, rows], device)

    def y_q(h, device, slot):
        rows = pl.ds(SPLIT + tail * h, tail)
        return send(wq_ref.at[rows], wq_all.at[slot, rows], device)

    histR = {0: x_hist(0, xR, 2)}
    histL = {1: x_hist(1, xL, 1)}
    ykR = {0: y_k(0, yR, 1)}
    ykL = {1: y_k(1, yL, 0)}
    metaR = send(meta_ref, meta_all.at[2, 0], xR)
    metaL = send(meta_ref, meta_all.at[1, 0], xL)
    send(meta_ref, meta_all.at[0, 1], other)
    load(meta_ref, meta_all.at[0, 0])
    load(hist_ref, hist_all.at[0, 0])

    load_x.wait()
    for r in range(4):
        onehot = (
            lax.broadcasted_iota(jnp.int32, (128, 32), 0) == kept_ref[pl.ds(r, 1), :]
        ).astype(F32).astype(BF16)
        sel_v[r] = dot(onehot, x_v[r], TN).astype(BF16)
    selR = {0: x_sel(0, xR, 2)}
    selL = {1: x_sel(1, xL, 1)}
    load(sel_v, sel_all.at[0, 0])

    load_wv.wait()
    head_of = lax.broadcasted_iota(jnp.int32, (16, 512), 1) // 64
    row_of = lax.broadcasted_iota(jnp.int32, (16, 512), 0)
    rating = jnp.where(head_of == row_of, rat_ref[...].astype(F32), 0.0).astype(BF16)
    wr_v[...] = dot(rating, wv_v[...], NT).astype(BF16)
    load(wr_v, wr_all.at[3])

    zsR.wait_recv()
    zsL.wait_recv()
    gA, gB = pl.ds(0, 2), pl.ds(2, 1)

    def z_send(group, step, device, start=0, size=SLICE):
        rows = zrows(step, start, size)
        return send(wq_all.at[group, rows], wq_all.at[group, rows], device)

    aR = [z_send(gA, 0, zR)]
    aL = [z_send(gA, 0, zL)]
    zs2R = send(wq_all.at[1, zrows(0, 0, half)], wq_all.at[2, zrows(0, 0, half)], yR)
    zs2L = send(wq_all.at[0, zrows(0, half, half)], wq_all.at[2, zrows(0, half, half)], yL)
    yqR = {0: y_q(0, yR, 1)}
    yqL = {1: y_q(1, yL, 0)}
    wrR = send(wr_v, wr_all.at[1], yR)
    wrL = send(wr_v, wr_all.at[0], yL)
    histR[1], histL[0] = x_hist(1, xR, 2), x_hist(0, xL, 1)
    selR[1], selL[0] = x_sel(1, xR, 2), x_sel(0, xL, 1)
    ykR[1], ykL[0] = y_k(1, yR, 1), y_k(0, yL, 0)
    yqR[1], yqL[0] = y_q(1, yR, 1), y_q(0, yL, 0)
    send(hist_ref, hist_all.at[0, 1], other)
    send(sel_v, sel_all.at[0, 1], other)

    load_w1.wait()

    @pl.loop(0, 4)
    def _(r):
        rows = pl.ds(pl.multiple_of(r * 128, 128), 128)
        block = x_v[r]
        scores = jnp.zeros((128, 1), F32)
        for q in range(4):
            cols = pl.ds(256 * q, 256)
            hidden = jnp.maximum(dot(block, w1_v[:, cols]), 0.0)
            hid_v[rows, cols] = hidden
            scores = scores + jnp.sum(hidden * v_ref[:, cols], axis=1, keepdims=True)
        weights = jnp.exp(scores)
        st_v[rows, :] = jnp.broadcast_to(weights / jnp.sum(weights, axis=0, keepdims=True), (128, 128))
        xt_v[:, rows] = block.T

    load(hid_v, hid_out)
    load(st_v, st_out)
    load(xt_v, xt_out)

    def x_forward(kind, ref, h, arrived):
        arrived.wait_recv()
        rows = pl.ds(2 * h, 2)
        device, slot = (xR, 2) if h == 0 else (xL, 1)
        piece = ref.at[slot, 0, rows]
        on = send(piece, ref.at[3, 0, rows], device)
        send(piece, ref.at[slot, 1, rows], other)
        return on

    def x_across(ref, slot, h, arrived):
        arrived.wait_recv()
        rows = pl.ds(2 * h, 2)
        send(ref.at[slot, 0, rows], ref.at[slot, 1, rows], other)

    metaR.wait_recv()
    metaL.wait_recv()
    meta2 = send(meta_all.at[2, 0], meta_all.at[3, 0], xR)
    send(meta_all.at[2, 0], meta_all.at[2, 1], other)
    send(meta_all.at[1, 0], meta_all.at[1, 1], other)
    zs2R.wait_recv()
    zs2L.wait_recv()
    bR = [z_send(gB, 0, zR)]
    bL = [z_send(gB, 0, zL)]
    hist2R = x_forward("h", hist_all, 0, histR[0])
    hist2L = x_forward("h", hist_all, 1, histL[1])
    aR[0].wait_recv()
    aR.append(z_send(gA, -1, zR))
    aL[0].wait_recv()
    aL.append(z_send(gA, 1, zL))
    sel2R = x_forward("s", sel_all, 0, selR[0])
    sel2L = x_forward("s", sel_all, 1, selL[1])
    bR[0].wait_recv()
    bR.append(z_send(gB, -1, zR))
    bL[0].wait_recv()
    bL.append(z_send(gB, 1, zL))

    def y_forward(h, ak, aq):
        device, slot = (yR, 1) if h == 0 else (yL, 0)
        ak.wait_recv()
        rows = pl.ds(256 * h, 256)
        k2 = send(wk_all.at[slot, rows], wk_all.at[2, rows], device)
        aq.wait_recv()
        rows = pl.ds(SPLIT + tail * h, tail)
        q2 = send(wq_all.at[slot, rows], wq_all.at[2, rows], device)
        return [k2, q2]

    last = y_forward(0, ykR[0], yqR[0]) + y_forward(1, ykL[1], yqL[1])
    aR[1].wait_recv()
    aR.append(z_send(gA, -2, zR))
    aL[1].wait_recv()
    aL.append(z_send(gA, 2, zL))
    wrR.wait_recv()
    wrL.wait_recv()
    last.append(send(wr_all.at[1], wr_all.at[2], yR))
    bR[1].wait_recv()
    bR.append(z_send(gB, -2, zR))
    bL[1].wait_recv()
    bL.append(z_send(gB, 2, zL))
    meta2.wait_recv()
    send(meta_all.at[3, 0], meta_all.at[3, 1], other)
    x_across(hist_all, 2, 1, histR[1])
    x_across(hist_all, 1, 0, histL[0])
    aR[2].wait_recv()
    aR.append(z_send(gA, -3, zR, 0, half))
    aL[2].wait_recv()
    aL.append(z_send(gA, 3, zL, half, half))
    x_across(sel_all, 2, 1, selR[1])
    x_across(sel_all, 1, 0, selL[0])
    bR[2].wait_recv()
    bR.append(z_send(gB, -3, zR, 0, half))
    bL[2].wait_recv()
    bL.append(z_send(gB, 3, zL, half, half))
    x_across(hist_all, 3, 0, hist2R)
    x_across(hist_all, 3, 1, hist2L)
    x_across(sel_all, 3, 0, sel2R)
    x_across(sel_all, 3, 1, sel2L)

    waited = {
        id(c)
        for c in (
            zsR, zsL, zs2R, zs2L, metaR, metaL, meta2, wrR, wrL, hist2R, hist2L, sel2R, sel2L,
            *histR.values(), *histL.values(), *selR.values(), *selL.values(),
            ykR[0], ykL[1], yqR[0], yqL[1], *aR[:3], *aL[:3], *bR[:3], *bL[:3],
        )
    }
    for copy in used:
        if id(copy) not in waited:
            copy.wait_recv()
    for copy in used:
        copy.wait_send()
    for copy in local:
        if all(copy is not done for done in (load_x, load_wv, load_w1)):
            copy.wait()


def ranker_kernel(
    meta_ref, sel_ref, hist_ref, wq_ref, wk_ref, wq_own, wk_own, wr_ref, out_ref,
    sel_v, hist_v, wq_v, wk_v, wr_v, wide_v, acc_v, list_s, in_sem, w_sem,
):
    x, y, c = lax.axis_index(GX), lax.axis_index(GY), lax.axis_index(GC)
    copies = [
        pltpu.make_async_copy(hist_ref, hist_v, in_sem.at[0]),
        pltpu.make_async_copy(sel_ref, sel_v, in_sem.at[1]),
        pltpu.make_async_copy(wr_ref, wr_v, in_sem.at[2]),
    ]
    weights = []
    for d in range(4):
        if d == 3:
            pair = (wq_own, wk_own)
        else:
            pair = (wq_ref.at[d], wk_ref.at[d])
        weights.append(
            (
                pltpu.make_async_copy(pair[0], wq_v.at[d], w_sem.at[d, 0]),
                pltpu.make_async_copy(pair[1], wk_v.at[d], w_sem.at[d, 1]),
            )
        )
    weights[0][0].start()
    weights[0][1].start()
    for copy in copies:
        copy.start()
    for d in range(1, 4):
        weights[d][0].start()
        weights[d][1].start()
    acc_v[...] = jnp.zeros_like(acc_v)
    for copy in copies:
        copy.wait()

    head_of = lax.broadcasted_iota(jnp.int32, (32, 512), 1) // 64
    slot_row = lax.broadcasted_iota(jnp.int32, (128, 256), 0)

    @pl.loop(0, 4)
    def _(d):
        step = jnp.where(d == 3, 0, jnp.where(d == 2, 2, jnp.where(d == 1, 3, 1)))
        expert = (x * 4 + lax.rem(y + step, 4)) * 2 + c

        def listed(r, count):
            here = lax.shift_right_logical(meta_ref[(r // 4) * 8, lax.rem(r, 4)], expert) & 1
            list_s[count] = r
            return count + here

        count = lax.fori_loop(0, 32, listed, jnp.int32(0))
        for k in range(3):
            list_s[count + k] = 32

        pltpu.make_async_copy(wq_own, wq_v.at[d], w_sem.at[d, 0]).wait()
        pltpu.make_async_copy(wk_own, wk_v.at[d], w_sem.at[d, 1]).wait()
        small = wr_v[d].astype(F32)
        for h in range(HEADS):
            wide_v[pl.ds(32 * h, 32), :] = jnp.broadcast_to(small[h : h + 1, :], (32, 512)).astype(BF16)

        @pl.loop(0, lax.div(count + 3, 4))
        def _(chunk):
            ids = [list_s[chunk * 4 + k] for k in range(4)]
            safe = [jnp.minimum(i, 31) for i in ids]
            rows = jnp.concatenate([sel_v[i] for i in safe], axis=0)
            queries = dot(rows, wq_v[d]).astype(BF16)
            slots = jnp.concatenate([hist_v[i] for i in safe], axis=0)
            keys = dot(slots, wk_v[d]).astype(BF16)
            worth = dot(slots, wide_v[...], NT)
            for k in range(4):
                length = meta_ref[(safe[k] // 4) * 8, 4 + lax.rem(safe[k], 4)]
                mine = queries[32 * k : 32 * k + 32]
                spread = jnp.concatenate(
                    [jnp.where(head_of == h, mine, jnp.zeros_like(mine)) for h in range(HEADS)], axis=0
                )
                logits = dot(keys[128 * k : 128 * k + 128], spread, NT) * 0.125
                w = jnp.where(slot_row < length, jnp.exp(logits), 0.0)
                top = jnp.sum(w * worth[128 * k : 128 * k + 128], axis=0, keepdims=True)
                score = top / jnp.sum(w, axis=0, keepdims=True)
                score = score[:, :128] + score[:, 128:]
                score = score + pltpu.roll(score, 64, 1)
                score = score + pltpu.roll(score, 32, 1)
                acc_v[pl.ds(ids[k], 1), :] += score

    for s in range(8):
        out_ref[s, pl.ds(0, 4), :] = acc_v[pl.ds(4 * s, 4), :]
        out_ref[s, pl.ds(4, 4), :] = jnp.zeros((4, 128), F32)


def reduce_kernel(
    part_ref, kept_ref, v_ref, st_ref, hid_ref, xt_ref,
    gh_ref, gs_ref,
    hid_v, xt_v, hg_v, t_v, ga_s, ga_r, own_v, b1_s, b1_r, b2_s, b2_r, a1_v, a2_v,
    c1_s, c1_r, c2_s, c2_r, fin_v, d_s, d_r, e_v, s0_v, sx_v, sy_v, sz_v, send_sem, recv_sem, load_sem,
):
    x, y, z, c = (lax.axis_index(a) for a in (GX, GY, GZ, GC))
    other = {GC: 1 - c}
    used = []

    def send(src, dst, device):
        k = len(used)
        copy = pltpu.make_async_remote_copy(
            src_ref=src, dst_ref=dst, send_sem=send_sem.at[k], recv_sem=recv_sem.at[k],
            device_id=device, device_id_type=MESH,
        )
        copy.start()
        used.append(copy)
        return copy

    load_h = pltpu.make_async_copy(hid_ref, hid_v.at[pl.ds(0, 512)], load_sem.at[0])
    load_h.start()
    load_x = pltpu.make_async_copy(xt_ref, xt_v, load_sem.at[1])
    load_x.start()

    xs = [at(GX, k, NX) for k in (1, 2, 3)]
    ys = [at(GY, k, NY) for k in (1, 2, 3)]
    zs = [at(GZ, k, NZ) for k in range(1, NZ)]
    diag = [{**d, **other} for d in xs]
    peers = [*xs, *ys, *zs, *diag, other]
    barrier = pltpu.get_barrier_semaphore()
    for peer in peers:
        pl.semaphore_signal(barrier, inc=1, device_id=peer, device_id_type=MESH)
    pl.semaphore_wait(barrier, len(peers))

    back = []
    slot_of = {1: 1, 2: 3, 3: 2}
    for k in (1, 2, 3):
        s = slot_of[k]
        back.append(send(part_ref.at[2 * s], t_v.at[2 * s], xs[k - 1]))
        back.append(send(part_ref.at[2 * s + 1], t_v.at[2 * s + 1], diag[k - 1]))
    back.append(send(part_ref.at[1], t_v.at[1], other))
    t_v[0] = part_ref[0]
    load_h.wait()
    load_x.wait()
    for copy in back:
        copy.wait_recv()
    teacher = t_v[0]
    for k in range(1, 8):
        teacher = teacher + t_v[k]
    live = lax.broadcasted_iota(jnp.int32, (8, 128), 1) < 32
    risen = jnp.where(live, jnp.exp(teacher / 6.0), 0.0)
    t_v[0] = risen / jnp.sum(risen, axis=1, keepdims=True)

    for r in range(4):
        rows = pl.ds(128 * r, 128)
        spots = lax.broadcasted_iota(jnp.int32, (128, 32), 0) == kept_ref[pl.ds(r, 1), :]
        aim = jnp.sum(jnp.where(spots, t_v[0, pl.ds(r, 1), pl.ds(0, 32)], 0.0), axis=1, keepdims=True)
        grad = st_ref[rows, pl.ds(0, 1)] - aim
        for q in range(4):
            cols = pl.ds(256 * q, 256)
            hidden = hid_v[rows, cols]
            hg_v[rows, cols] = jnp.where(hidden > 0.0, grad * v_ref[:, cols], 0.0).astype(BF16)
            hid_v[pl.ds(512 + 8 * r, 8), cols] = jnp.sum((grad * hidden).reshape(16, 8, 256), axis=0)
    total = hid_v[pl.ds(512, 8), :] + hid_v[pl.ds(520, 8), :] + hid_v[pl.ds(528, 8), :] + hid_v[pl.ds(536, 8), :]
    row = jnp.sum(total, axis=0, keepdims=True)
    for k in range(8):
        s0_v[0, pl.ds(k, 1), :] = row[:, 128 * k : 128 * k + 128]
    sa = send(s0_v.at[0], s0_v.at[1], other)

    core = []

    def rows_of(k, side):
        return xt_v[pl.ds(4 * k, 4), side].reshape(128, 512)

    for k in range(4):
        ga_s[pl.ds(4 * k, 4)] = dot(rows_of(k, 1 - c), hg_v[...]).astype(BF16).reshape(4, 32, 1024)
        core.append(send(ga_s.at[pl.ds(4 * k, 4)], ga_r.at[pl.ds(4 * k, 4)], other))
    for k in range(4):
        own_v[pl.ds(4 * k, 4)] = dot(rows_of(k, c), hg_v[...]).reshape(4, 32, 1024)
    for k in range(4):
        core[k].wait_recv()
        blocks = pl.ds(4 * k, 4)
        own_v[blocks] = own_v[blocks] + ga_r[blocks].astype(F32)
    sa.wait_recv()
    sx_v[x] = s0_v[0] + s0_v[1]

    n1, n2 = pl.ds(0, 512), pl.ds(512, 512)
    first, second, sb = [], [], []
    for k in (2, 1, 3):
        tx, ty = xs[k - 1][GX], ys[k - 1][GY]
        b1_s[k - 1] = own_v[pl.ds(4 * tx, 4), :, n1].astype(BF16)
        first.append(send(b1_s.at[k - 1], b1_r.at[k - 1], xs[k - 1]))
        for j in range(4):
            b2_s[k - 1, j] = own_v[4 * j + ty, :, n2].astype(BF16)
        second.append(send(b2_s.at[k - 1], b2_r.at[k - 1], ys[k - 1]))
        sb.append(send(sx_v.at[x], sx_v.at[x], xs[k - 1]))
    for copy in sb:
        copy.wait_recv()
    sy_v[y] = (sx_v[0] + sx_v[1]) + (sx_v[2] + sx_v[3])
    sc = [send(sy_v.at[y], sy_v.at[y], ys[k]) for k in range(3)]
    for copy in first:
        copy.wait_recv()
    a1_v[...] = own_v[pl.ds(4 * x, 4), :, n1] + (
        b1_r[0].astype(F32) + b1_r[1].astype(F32) + b1_r[2].astype(F32)
    )
    third = []
    for k in (2, 1, 3):
        c1_s[k - 1] = a1_v[ys[k - 1][GY]].astype(BF16)
        third.append(send(c1_s.at[k - 1], c1_r.at[k - 1], ys[k - 1]))
    for copy in second:
        copy.wait_recv()
    for j in range(4):
        a2_v[j] = own_v[4 * j + y, :, n2] + (
            b2_r[0, j].astype(F32) + b2_r[1, j].astype(F32) + b2_r[2, j].astype(F32)
        )
    for k in (2, 1, 3):
        c2_s[k - 1] = a2_v[xs[k - 1][GX]].astype(BF16)
        third.append(send(c2_s.at[k - 1], c2_r.at[k - 1], xs[k - 1]))
    for copy in sc:
        copy.wait_recv()
    sz_v[z] = (sy_v[0] + sy_v[1]) + (sy_v[2] + sy_v[3])
    sd = [send(sz_v.at[z], sz_v.at[z], zs[k]) for k in range(NZ - 1)]
    for copy in third:
        copy.wait_recv()
    fin1 = a1_v[y] + (c1_r[0].astype(F32) + c1_r[1].astype(F32) + c1_r[2].astype(F32))
    fin2 = a2_v[x] + (c2_r[0].astype(F32) + c2_r[1].astype(F32) + c2_r[2].astype(F32))
    for k in range(4):
        fin_v[k] = fin1[:, 128 * k : 128 * k + 128]
        fin_v[4 + k] = fin2[:, 128 * k : 128 * k + 128]
    d_s[...] = fin_v[...].astype(BF16)

    fourth = []
    for k in (4, 3, 5, 2, 6, 1, 7):
        fourth.append(send(d_s.at[zs[k - 1][GZ]], d_r.at[k - 1], zs[k - 1]))
    for copy in fourth:
        copy.wait_recv()
    whole = fin_v[z]
    for k in range(NZ - 1):
        whole = whole + d_r[k].astype(F32)
    e_v[z] = whole
    fifth = [send(e_v.at[z], e_v.at[z], zs[k - 1]) for k in (4, 3, 5, 2, 6, 1, 7)]
    for copy in sd:
        copy.wait_recv()
    gs = sz_v[0]
    for k in range(1, NZ):
        gs = gs + sz_v[k]
    gs_ref[...] = gs
    for copy in fifth:
        copy.wait_recv()
    for k in range(NZ):
        gh_ref[:, pl.ds(128 * k, 128)] = e_v[k]
    for copy in used:
        copy.wait_send()


def any_specs(n):
    return [pl.BlockSpec(memory_space=pl.ANY)] * n


def vmem_specs(n):
    return [pl.BlockSpec(memory_space=pltpu.VMEM)] * n


def shapes(*items):
    return [jax.ShapeDtypeStruct(s, t) for s, t in items]


def body(
    offer_attribute_matrix,
    kept_offers,
    expert_target,
    sequence_extent,
    behaviour_sequence,
    inner_projection_matrix,
    student_rating_vector,
    asking_matrix,
    lookup_matrix,
    content_matrix,
    expert_rating_vector,
):
    bits = jnp.sum(jnp.left_shift(jnp.int32(1), expert_target), axis=1)
    info = jnp.concatenate([bits, sequence_extent])
    meta = jnp.zeros((8, 128), jnp.int32).at[0, :8].set(info)
    v_row = student_rating_vector.astype(F32).reshape(1, 1024)
    wq, wk, wv = asking_matrix[0], lookup_matrix[0], content_matrix[0]

    sel_all, hist_all, meta_all, wq_all, wk_all, wr_all, hidden, student, turned = pl.pallas_call(
        gather_kernel,
        out_shape=shapes(
            ((4, 2, 4, 32, 1024), BF16),
            ((4, 2, 4, 128, 512), BF16),
            ((4, 2, 8, 128), jnp.int32),
            ((3, 1024, 512), BF16),
            ((3, 512, 512), BF16),
            ((4, 16, 512), BF16),
            ((512, 1024), F32),
            ((512, 128), F32),
            ((1024, 512), BF16),
        ),
        in_specs=[
            *any_specs(1), *vmem_specs(1), *any_specs(1), *vmem_specs(1), *any_specs(4), *vmem_specs(1),
            *any_specs(1),
        ],
        out_specs=any_specs(9),
        scratch_shapes=[
            pltpu.VMEM((4, 128, 1024), BF16),
            pltpu.VMEM((1024, 1024), BF16),
            pltpu.VMEM((512, 512), BF16),
            pltpu.VMEM((4, 32, 1024), BF16),
            pltpu.VMEM((16, 512), BF16),
            pltpu.VMEM((512, 1024), F32),
            pltpu.VMEM((512, 128), F32),
            pltpu.VMEM((1024, 512), BF16),
            pltpu.SemaphoreType.DMA((80,)),
            pltpu.SemaphoreType.DMA((80,)),
            pltpu.SemaphoreType.DMA((12,)),
        ],
        compiler_params=pltpu.CompilerParams(
            collective_id=0, has_side_effects=True, vmem_limit_bytes=40 * 2**20
        ),
        name="gather_requests_and_experts",
    )(
        offer_attribute_matrix, kept_offers, inner_projection_matrix, v_row, behaviour_sequence,
        wq, wk, wv, expert_rating_vector, meta,
    )

    part = pl.pallas_call(
        ranker_kernel,
        out_shape=jax.ShapeDtypeStruct((8, 8, 128), F32),
        in_specs=[pl.BlockSpec(memory_space=pltpu.SMEM), *any_specs(7)],
        out_specs=pl.BlockSpec(memory_space=pltpu.VMEM),
        scratch_shapes=[
            pltpu.VMEM((32, 32, 1024), BF16),
            pltpu.VMEM((32, 128, 512), BF16),
            pltpu.VMEM((4, 1024, 512), BF16),
            pltpu.VMEM((4, 512, 512), BF16),
            pltpu.VMEM((4, 16, 512), BF16),
            pltpu.VMEM((256, 512), BF16),
            pltpu.VMEM((40, 128), F32),
            pltpu.SMEM((40,), jnp.int32),
            pltpu.SemaphoreType.DMA((3,)),
            pltpu.SemaphoreType.DMA((4, 2)),
        ],
        compiler_params=pltpu.CompilerParams(vmem_limit_bytes=48 * 2**20),
        name="rankers",
    )(
        meta_all.reshape(64, 128), sel_all.reshape(32, 32, 1024), hist_all.reshape(32, 128, 512),
        wq_all, wk_all, wq, wk, wr_all,
    )

    grad_hidden, grad_score = pl.pallas_call(
        reduce_kernel,
        out_shape=shapes(((32, 1024), F32), ((8, 128), F32)),
        in_specs=[*vmem_specs(4), *any_specs(2)],
        out_specs=vmem_specs(2),
        scratch_shapes=[
            pltpu.VMEM((544, 1024), F32),
            pltpu.VMEM((16, 2, 32, 512), BF16),
            pltpu.VMEM((512, 1024), BF16),
            pltpu.VMEM((8, 8, 128), F32),
            pltpu.VMEM((16, 32, 1024), BF16),
            pltpu.VMEM((16, 32, 1024), BF16),
            pltpu.VMEM((16, 32, 1024), F32),
            *[pltpu.VMEM((3, 4, 32, 512), BF16) for _ in range(4)],
            *[pltpu.VMEM((4, 32, 512), F32) for _ in range(2)],
            *[pltpu.VMEM((3, 32, 512), BF16) for _ in range(4)],
            pltpu.VMEM((8, 32, 128), F32),
            pltpu.VMEM((8, 32, 128), BF16),
            pltpu.VMEM((7, 32, 128), BF16),
            pltpu.VMEM((8, 32, 128), F32),
            pltpu.VMEM((2, 8, 128), F32),
            pltpu.VMEM((4, 8, 128), F32),
            pltpu.VMEM((4, 8, 128), F32),
            pltpu.VMEM((8, 8, 128), F32),
            pltpu.SemaphoreType.DMA((64,)),
            pltpu.SemaphoreType.DMA((64,)),
            pltpu.SemaphoreType.DMA((2,)),
        ],
        compiler_params=pltpu.CompilerParams(
            collective_id=1, has_side_effects=True, vmem_limit_bytes=40 * 2**20
        ),
        name="targets_and_gradients",
    )(part, kept_offers, v_row, student, hidden, turned.reshape(16, 2, 32, 512))
    return grad_hidden, grad_score.reshape(1024)


def solution(mesh):
    torus = Mesh(mesh.devices.reshape(mesh.shape["group"], NX, NY, 2), GROUP_SHARD)
    return jax.shard_map(
        body,
        mesh=torus,
        in_specs=(
            P(GROUP_SHARD, None, None),
            P(GROUP_SHARD, None),
            P(GROUP_SHARD, None),
            P(GROUP_SHARD),
            P(GROUP_SHARD, None, None),
            P(),
            P(),
            P(SHARD, None, None),
            P(SHARD, None, None),
            P(SHARD, None, None),
            P(SHARD, None),
        ),
        out_specs=(P(SHARD, None), P()),
        check_vma=False,
    )
```

time: 465 us -> 105 us (0.23)
  waiting for transfers between devices: 141 us -> 0 us
  blocking collectives: 113 us -> 0 us
  Pallas kernels: 0 us -> 92.2 us
  matrix products: 68.6 us -> 0 us
  local copies, waits for them, and re-layouts: 71.1 us -> 9.8 us
  starting transfers between devices: 58.1 us -> 0 us
  other arithmetic: 8.46 us -> 2.21 us
    all_to_all x5 -> x0, waiting for transfers between devices: 141 us -> none  [the longest x1 102 us: body(): lax.all_to_all(send_hist, SHARD, split_axis=0, concat_axis=0, tiled=True)]
    pallas_call x0 -> x3, Pallas kernels: none -> 92.2 us  [the longest x1 42 us: body(): pl.pallas_call(gather_kernel, out_shape=shapes(((4, 2, 4, 32, 1024), BF16...]
    dot_general x27 -> x0, matrix products: 68.6 us -> none  [the longest x4 23.8 us: ranker_block(): jnp.einsum('skhd,sjhd->shkj', queries, key_rows, preferred_element_type=j...]
    all_to_all x5 -> x0, starting transfers between devices: 58.1 us -> none  [the longest x1 25.2 us: turned_blocks(): result = lax.all_to_all(result, axes[k], k, k, tiled=True)]
    all_to_all x2 -> x0, blocking collectives: 56.8 us -> none  [the longest x1 53.1 us: sum_at_owner(): lax.all_to_all(blocks, axis, split_axis=0, concat_axis=0, tiled=True)]
    psum x4 -> x0, blocking collectives: 56.5 us -> none  [one_axis_at_a_time(): return functools.reduce(lax.psum, axes, value)]
    reshape x13 -> x0, local copies, waits for them, and re-layouts: 31.7 us -> none  [the longest x4 14.7 us: ranker_block(): key_rows.astype(jnp.bfloat16)]
    convert_element_type x6 -> x0, local copies, waits for them, and re-layouts: 15.9 us -> none  [the longest x1 11.3 us: body(): send_hist = jnp.einsum('rts,rjf->sjf', placing_b, behaviour_sequence, pre...]
  transfers between devices with their start and end apart: 5 -> 0, of which waited for: 3 -> 0; matrix products, arithmetic and copies ran while one was open for 6% -> 0% of each run, Pallas kernels for 0% -> 0%
where the time goes in v1:
time: 105 us
  Pallas kernels  92.2 us (88%)
  local copies, waits for them, and re-layouts  9.8 us (9%)
  other arithmetic  2.21 us (2%)
    pallas_call x1, Pallas kernels, body(): pl.pallas_call(gather_kernel, out_shape=shapes(((4, 2, 4, 32, 1024), BF16...  42 us
    pallas_call x1, Pallas kernels, body(): pl.pallas_call(reduce_kernel, out_shape=shapes(((32, 1024), F32), ((8, 12...  39.4 us
    pallas_call x1, Pallas kernels, body(): pl.pallas_call(ranker_kernel, out_shape=jax.ShapeDtypeStruct((8, 8, 128),...  10.8 us
    unnamed x24, local copies, waits for them, and re-layouts  9.79 us

profile of v1, /device:TPU:2, one launch (start us, length us, event | category | flops | bytes accessed | tf_op | source)
XLA Modules:
  0.0 104.9 jit_solution(14070365491221377982)
XLA Ops:
  0.6 0.8 shift-left_reduce_fusion
  1.4 0.7 add_bitcast_fusion
  2.2 0.7 reshape.62
  2.9 0.0 copy-start
  2.9 1.2 %copy-done = bf16[1,1024,512]{2,1,0:T(8,128)(2,1)S(1)} copy-done((bf16[1,1024,512]{2,1,0:T(8,128)(2,1)S(1)}, bf16[1,1024,512]{2,1,0:T(8,128)(2,1)}, u32[]{:S(2)}) %copy-start) | copy-done | bytes 1048600
  4.1 0.0 copy-start.2
  4.1 1.6 %copy-done.2 = bf16[1024,1024]{1,0:T(8,128)(2,1)S(1)} copy-done((bf16[1024,1024]{1,0:T(8,128)(2,1)S(1)}, bf16[1024,1024]{1,0:T(8,128)(2,1)}, u32[]{:S(2)}) %copy-start.2) | copy-done | bytes 2097176
  5.7 0.0 copy-start.3
  5.7 1.0 copy-done.3
  6.7 0.0 copy-start.5
  6.7 1.2 %copy-done.5 = bf16[4,128,1024]{2,1,0:T(8,128)(2,1)S(1)} copy-done((bf16[4,128,1024]{2,1,0:T(8,128)(2,1)S(1)}, bf16[4,128,1024]{2,1,0:T(8,128)(2,1)}, u32[]{:S(2)}) %copy-start.5) | copy-done | bytes 1048600
  7.9 0.0 copy-start.6
  7.9 1.0 copy-done.6
  9.0 0.0 copy-start.7
  9.0 1.0 copy-done.7
  10.0 0.0 copy-start.8
  10.0 0.7 copy-done.8
  10.7 0.0 copy-start.10
  10.7 0.7 copy-done.10
  11.4 0.0 copy-start.1
  11.4 0.0 copy-start.4
  11.4 42.0 %gather_requests_and_experts.1 = (bf16[4,2,4,32,1024]{4,3,2,1,0:T(8,128)(2,1)S(1)}, bf16[4,2,4,128,512]{4,3,2,1,0:T(8,128)(2,1)}, s32[4,2,8,128]{3,2,1,0:T(8,128...) custom-call(bf16[4,128,1024]{2,1,0:T(8,128)(2,1)S(1)} %copy-done.5, ...), custom_call_target="tpu_custom_call" | custom-call | tf_op jit(solution)/shard_map/gather_requests_and_experts/pallas_call | solution.py:534
  53.4 0.0 copy-done.1
  53.4 0.0 copy-done.4
  53.4 0.0 copy-start.9
  53.4 10.8 %rankers.1.part_ref = f32[8,8,128]{2,1,0:T(8,128)S(1)} custom-call(s32[64,128]{1,0:T(8,128)S(1)} %bitcast.20, bf16[32,32,1024]{2,1,0:T(8,128)(2,1)S(1)} %bitcast.13, bf16[32,128,512]{2,1,0:T(8,128)(2,1)} %bitcast.22, bf16[3,1024,512]{2,1,0:T(8,128)(2,1)} %get-tuple-element.28.wq_ref, bf16[3,512,512]{2,1,0:T(8,128)(2,1)S(1)} %get-tuple-element.29.wk_ref, ...), custom_call_target="tpu_custom_call" | custom-call | tf_op jit(solution)/shard_map/rankers/pallas_call | solution.py:574
  64.3 0.0 copy-done.9
  64.3 39.4 %targets_and_gradients.1 = (f32[32,1024]{1,0:T(8,128)S(1)}, f32[8,128]{1,0:T(8,128)S(1)}) custom-call(f32[8,8,128]{2,1,0:T(8,128)S(1)} %rankers.1.part_ref, s32[4,32]{1,0:T(4,128)S(1)} %copy-done.9, f32[1,1024]{1,0:T(1,128)S(1)} %bitcast.19, f32[512,128]{1,0:T(8,128)S(1)} %get-tuple-element.31.st_ref, f32[512,1024]{1,0:T(8,128)S(1)} %get-tuple-element.32.hid_ref, ...), custom_call_target="tpu_custom_call" | custom-call | tf_op jit(solution)/shard_map/targets_and_gradients/pallas_call | solution.py:598
  103.7 0.7 copy.15
  104.3 0.6 copy.16
  (1 shorter events, 0.0 us)
Async XLA Ops:
  2.9 1.2 %copy-start = (bf16[1,1024,512]{2,1,0:T(8,128)(2,1)S(1)}, bf16[1,1024,512]{2,1,0:T(8,128)(2,1)}, u32[]{:S(2)}) copy-start(bf16[1,1024,512]{2,1,0:T(8,128)(2,1)} %param.20) | copy-start | bytes 3145732
  4.1 1.6 %copy-start.2 = (bf16[1024,1024]{1,0:T(8,128)(2,1)S(1)}, bf16[1024,1024]{1,0:T(8,128)(2,1)}, u32[]{:S(2)}) copy-start(bf16[1024,1024]{1,0:T(8,128)(2,1)} %w1_ref.1) | copy-start | bytes 6291460
  5.7 1.0 copy-start.3
  6.7 1.2 %copy-start.5 = (bf16[4,128,1024]{2,1,0:T(8,128)(2,1)S(1)}, bf16[4,128,1024]{2,1,0:T(8,128)(2,1)}, u32[]{:S(2)}) copy-start(bf16[4,128,1024]{2,1,0:T(8,128)(2,1)} %x_ref.1) | copy-start | bytes 3145732
  7.9 1.0 copy-start.6
  9.0 1.0 copy-start.7
  10.0 0.7 copy-start.8
  10.7 0.7 copy-start.10
  11.4 42.0 %copy-start.1 = (bf16[1,1024,512]{2,1,0:T(8,128)(2,1)S(1)}, bf16[1,1024,512]{2,1,0:T(8,128)(2,1)}, u32[]{:S(2)}) copy-start(bf16[1,1024,512]{2,1,0:T(8,128)(2,1)} %param.20) | copy-start | bytes 3145732
  11.4 42.0 %copy-start.4 = (bf16[1,512,512]{2,1,0:T(8,128)(2,1)S(1)}, bf16[1,512,512]{2,1,0:T(8,128)(2,1)}, u32[]{:S(2)}) copy-start(bf16[1,512,512]{2,1,0:T(8,128)(2,1)} %param.21) | copy-start | bytes 1572868
  53.4 10.9 %copy-start.9 = (s32[4,32]{1,0:T(4,128)S(1)}, s32[4,32]{1,0:T(4,128)}, u32[]{:S(2)}) copy-start(s32[4,32]{1,0:T(4,128)} %kept_ref.3) | copy-start | bytes 1540

commit v2 on v0

v2 whole, which is shorter than its diff:
```python
import functools

import jax
import jax.numpy as jnp
from jax import lax
from jax.experimental import pallas as pl
from jax.experimental.pallas import tpu as pltpu
from jax.sharding import Mesh
from jax.sharding import PartitionSpec as P

MESH = pl.DeviceIdType.MESH
F32 = jnp.float32
BF16 = jnp.bfloat16
HEADS = 8
GZ, GX, GY, GC = "group", "shard_0", "shard_1", "shard_2"
SHARD = (GX, GY, GC)
GROUP_SHARD = (GZ, GX, GY, GC)
NX, NY, NZ = 4, 4, 8
SLICE = 96
SPLIT = SLICE * NZ
NT = (((1,), (1,)), ((), ()))
TN = (((0,), (0,)), ((), ()))


def dot(a, b, dims=(((1,), (0,)), ((), ()))):
    return lax.dot_general(a, b, dims, preferred_element_type=F32)


class Sent:
    def __init__(self, copy):
        self.copy, self.arrived = copy, False
        copy.start()

    def wait_recv(self):
        if not self.arrived:
            self.copy.wait_recv()
        self.arrived = True

    def wait_send(self):
        self.copy.wait_send()


def at(axis, step, size):
    return {axis: lax.rem(lax.axis_index(axis) + (step % size), size)}


def whole_kernel(
    x_ref, kept_in, target_in, extent_in, w1_ref, v_in, hist_ref, wq_ref, wk_ref, wv_ref, rat_in,
    gh_ref, gs_ref,
    sel0, sel1, sel2, sel3, hist0, hist1, hist2, hist3,
    meta_all, meta_s, wq_all, wk_all, wr_all, wide_v, acc_v,
    kept_ref, target_ref, extent_ref, v_ref, rat_ref,
    x_v, w1_v, wv_v, hid_v, st_v, xt_v, sum_v,
    hg_v, t_v, ga_s, ga_r, own_v, b1_s, b1_r, b2_s, b2_r, a1_v, a2_v,
    c1_s, c1_r, c2_s, c2_r, fin_v, d_s, d_r, e_v, s0_v, sx_v, sy_v, sz_v, send_sem, recv_sem, load_sem,
):
    sel_p, hist_p = (sel0, sel1, sel2, sel3), (hist0, hist1, hist2, hist3)
    x, y, z, c = (lax.axis_index(a) for a in (GX, GY, GZ, GC))
    other = {GC: 1 - c}
    used = []

    def send(src, dst, device):
        k = len(used)
        used.append(
            Sent(
                pltpu.make_async_remote_copy(
                    src_ref=src, dst_ref=dst, send_sem=send_sem.at[k], recv_sem=recv_sem.at[k],
                    device_id=device, device_id_type=MESH,
                )
            )
        )
        return used[-1]

    loads = []

    def load(src, dst):
        copy = pltpu.make_async_copy(src, dst, load_sem.at[len(loads)])
        copy.start()
        loads.append(copy)
        return copy

    load_small = [
        load(src, dst)
        for src, dst in (
            (target_in, target_ref), (extent_in, extent_ref), (kept_in, kept_ref), (rat_in, rat_ref),
            (v_in, v_ref),
        )
    ]
    load_x = load(x_ref, x_v)
    load_wv = load(wv_ref, wv_v)
    load_own = [load(hist_ref, hist0.at[0]), load(wq_ref, wq_all.at[0]), load(wk_ref, wk_all.at[0])]
    load_w1 = load(w1_ref, w1_v)

    xs = [at(GX, k, NX) for k in (1, 2, 3)]
    ys = [at(GY, k, NY) for k in (1, 2, 3)]
    zs = [at(GZ, k, NZ) for k in range(1, NZ)]
    diag = [{**d, **other} for d in xs]
    peers = [*xs, *ys, *zs, *diag, other]
    barrier = pltpu.get_barrier_semaphore()
    for peer in peers:
        pl.semaphore_signal(barrier, inc=1, device_id=peer, device_id_type=MESH)
    pl.semaphore_wait(barrier, len(peers))

    def zrows(step, start=0, size=SLICE):
        plane = lax.rem(z + (step % NZ), NZ)
        return pl.ds(pl.multiple_of(plane * SLICE + start, 16), size)

    half = SLICE // 2
    tail = (1024 - SPLIT) // 2
    xR, xL, yR, yL, zR, zL = xs[0], xs[2], ys[0], ys[2], zs[0], zs[6]

    zsR = send(wq_ref.at[zrows(0)], wq_all.at[2, zrows(0)], yR)
    zsL = send(wq_ref.at[zrows(0)], wq_all.at[1, zrows(0)], yL)

    def two(h):
        return pl.ds(2 * h, 2)

    def x_hist(h, device, slot):
        return send(hist_ref.at[two(h)], hist_p[slot].at[0, two(h)], device)

    def x_sel(h, device, slot):
        return send(sel0.at[0, two(h)], sel_p[slot].at[0, two(h)], device)

    def y_k(h, device, slot):
        rows = pl.ds(256 * h, 256)
        return send(wk_ref.at[rows], wk_all.at[slot, rows], device)

    def y_q(h, device, slot):
        rows = pl.ds(SPLIT + tail * h, tail)
        return send(wq_ref.at[rows], wq_all.at[slot, rows], device)

    histR, histL = {0: x_hist(0, xR, 2)}, {1: x_hist(1, xL, 1)}
    ykR, ykL = {0: y_k(0, yR, 2)}, {1: y_k(1, yL, 1)}
    for copy in load_small:
        copy.wait()
    bits = jnp.sum(jnp.left_shift(jnp.int32(1), target_ref[...]), axis=1, keepdims=True)
    meta_all[0, 0] = jnp.zeros((8, 128), jnp.int32)
    meta_all[0, 0, pl.ds(0, 4), :] = jnp.broadcast_to(bits, (4, 128))
    meta_all[0, 0, pl.ds(4, 1), pl.ds(0, 4)] = extent_ref[...]
    metaR = send(meta_all.at[0, 0], meta_all.at[2, 0], xR)
    metaL = send(meta_all.at[0, 0], meta_all.at[1, 0], xL)
    meta_on = [send(meta_all.at[0, 0], meta_all.at[0, 1], other)]

    load_x.wait()
    for r in range(4):
        onehot = (
            lax.broadcasted_iota(jnp.int32, (128, 32), 0) == kept_ref[pl.ds(r, 1), :]
        ).astype(F32).astype(BF16)
        sel0[0, r] = dot(onehot, x_v[r], TN).astype(BF16)
    selR, selL = {0: x_sel(0, xR, 2)}, {1: x_sel(1, xL, 1)}

    load_wv.wait()
    head_wide = lax.broadcasted_iota(jnp.int32, (16, 512), 1) // 64
    row_of = lax.broadcasted_iota(jnp.int32, (16, 512), 0)
    rating = jnp.where(head_wide == row_of, rat_ref[...].astype(F32), 0.0).astype(BF16)
    wr_all[0] = dot(rating, wv_v[...], NT).astype(BF16)
    wrR = send(wr_all.at[0], wr_all.at[2], yR)
    wrL = send(wr_all.at[0], wr_all.at[1], yL)

    zsR.wait_recv()
    zsL.wait_recv()
    gA, gB = pl.ds(1, 2), pl.ds(3, 1)

    def z_send(group, step, device, start=0, size=SLICE):
        rows = zrows(step, start, size)
        return send(wq_all.at[group, rows], wq_all.at[group, rows], device)

    aR, aL = [z_send(gA, 0, zR)], [z_send(gA, 0, zL)]
    zs2R = send(wq_all.at[2, zrows(0, 0, half)], wq_all.at[3, zrows(0, 0, half)], yR)
    zs2L = send(wq_all.at[1, zrows(0, half, half)], wq_all.at[3, zrows(0, half, half)], yL)
    yqR, yqL = {0: y_q(0, yR, 2)}, {1: y_q(1, yL, 1)}
    histR[1], histL[0] = x_hist(1, xR, 2), x_hist(0, xL, 1)
    selR[1], selL[0] = x_sel(1, xR, 2), x_sel(0, xL, 1)
    ykR[1], ykL[0] = y_k(1, yR, 2), y_k(0, yL, 1)
    yqR[1], yqL[0] = y_q(1, yR, 2), y_q(0, yL, 1)
    on = {0: [send(hist_ref, hist0.at[1], other), send(sel0.at[0], sel0.at[1], other)], 1: [], 2: [], 3: []}

    def tower(r):
        rows = pl.ds(128 * r, 128)
        block = x_v[r]
        scores = jnp.zeros((128, 1), F32)
        for q in range(4):
            cols = pl.ds(256 * q, 256)
            hidden = jnp.maximum(dot(block, w1_v[:, cols]), 0.0)
            hid_v[rows, cols] = hidden
            scores = scores + jnp.sum(hidden * v_ref[:, cols].astype(F32), axis=1, keepdims=True)
        weights = jnp.exp(scores)
        st_v[rows, :] = jnp.broadcast_to(weights / jnp.sum(weights, axis=0, keepdims=True), (128, 128))
        xt_v[:, rows] = block.T

    load_w1.wait()
    tower(0)

    def x_across(refs, slot, h, arrived):
        arrived.wait_recv()
        on[slot].append(send(refs[slot].at[0, two(h)], refs[slot].at[1, two(h)], other))

    def x_forward(refs, h, arrived):
        arrived.wait_recv()
        device, slot = (xR, 2) if h == 0 else (xL, 1)
        sent = send(refs[slot].at[0, two(h)], refs[3].at[0, two(h)], device)
        x_across(refs, slot, h, arrived)
        return sent

    def y_forward(h, ak, aq):
        device, slot = (yR, 2) if h == 0 else (yL, 1)
        ak.wait_recv()
        rows = pl.ds(256 * h, 256)
        send(wk_all.at[slot, rows], wk_all.at[3, rows], device)
        aq.wait_recv()
        rows = pl.ds(SPLIT + tail * h, tail)
        send(wq_all.at[slot, rows], wq_all.at[3, rows], device)

    metaR.wait_recv()
    metaL.wait_recv()
    meta2 = send(meta_all.at[2, 0], meta_all.at[3, 0], xR)
    meta_on.append(send(meta_all.at[2, 0], meta_all.at[2, 1], other))
    meta_on.append(send(meta_all.at[1, 0], meta_all.at[1, 1], other))
    zs2R.wait_recv()
    zs2L.wait_recv()
    bR, bL = [z_send(gB, 0, zR)], [z_send(gB, 0, zL)]
    tower(1)
    hist2R = x_forward(hist_p, 0, histR[0])
    hist2L = x_forward(hist_p, 1, histL[1])
    aR[0].wait_recv()
    aR.append(z_send(gA, -1, zR))
    aL[0].wait_recv()
    aL.append(z_send(gA, 1, zL))
    tower(2)
    sel2R = x_forward(sel_p, 0, selR[0])
    sel2L = x_forward(sel_p, 1, selL[1])
    wrR.wait_recv()
    wrL.wait_recv()
    wr2 = send(wr_all.at[2], wr_all.at[3], yR)
    meta2.wait_recv()
    meta_on.append(send(meta_all.at[3, 0], meta_all.at[3, 1], other))
    bR[0].wait_recv()
    bR.append(z_send(gB, -1, zR))
    bL[0].wait_recv()
    bL.append(z_send(gB, 1, zL))
    tower(3)
    y_forward(0, ykR[0], yqR[0])
    y_forward(1, ykL[1], yqL[1])
    aR[1].wait_recv()
    aR.append(z_send(gA, -2, zR))
    aL[1].wait_recv()
    aL.append(z_send(gA, 2, zL))
    bR[1].wait_recv()
    bR.append(z_send(gB, -2, zR))
    bL[1].wait_recv()
    bL.append(z_send(gB, 2, zL))
    for copy in meta_on:
        copy.wait_recv()
    info = [
        load(meta_all.at[k // 2, k % 2], meta_s.at[pl.ds(8 * k, 8)]) for k in range(8)
    ]
    acc_v[...] = jnp.zeros_like(acc_v)

    head_of = lax.broadcasted_iota(jnp.int32, (32, 512), 1) // 64
    slot_row = lax.broadcasted_iota(jnp.int32, (128, 256), 0)
    out_row = lax.broadcasted_iota(jnp.int32, (8, 128), 0)

    def ranked(d, p):
        step = jnp.where(d == 3, 2, jnp.where(d == 2, 3, jnp.where(d == 1, 1, 0)))
        expert = (x * 4 + lax.rem(y + step, 4)) * 2 + c
        places = []
        for core in range(2):
            base = 16 * p + 8 * core
            seen = jnp.int32(0)
            ids, found = [jnp.int32(0)] * 2, [jnp.int32(0)] * 2
            for i in range(4):
                here = lax.shift_right_logical(meta_s[base + i, 0], expert) & 1
                for j in range(2):
                    hit = jnp.where(seen == j, here, 0)
                    ids[j] = ids[j] + i * hit
                    found[j] = found[j] + hit
                seen = seen + here
            places += [(core, ids[j], found[j]) for j in range(2)]
        rows = jnp.concatenate([sel_p[p][core, i] for core, i, _ in places], axis=0)
        queries = dot(rows, wq_all[d]).astype(BF16)
        slots = jnp.concatenate([hist_p[p][core, i] for core, i, _ in places], axis=0)
        keys = dot(slots, wk_all[d]).astype(BF16)
        worth = dot(slots, wide_v[d])
        for k, (core, i, found) in enumerate(places):
            length = meta_s[16 * p + 8 * core + 4, i]
            mine = queries[32 * k : 32 * k + 32]
            spread = jnp.concatenate(
                [jnp.where(head_of == h, mine, jnp.zeros_like(mine)) for h in range(HEADS)], axis=0
            )
            logits = dot(keys[128 * k : 128 * k + 128], spread, NT) * 0.125
            w = jnp.where(slot_row < length, jnp.exp(logits), 0.0)
            top = jnp.sum(w * worth[128 * k : 128 * k + 128], axis=0, keepdims=True)
            score = top / jnp.sum(w, axis=0, keepdims=True)
            score = score[:, :128] + score[:, 128:]
            score = score + pltpu.roll(score, 64, 1)
            score = score + pltpu.roll(score, 32, 1)
            mark = out_row == jnp.where(found == 1, i, -1)
            acc_v[p, core] = acc_v[p, core] + jnp.where(mark, score, 0.0)

    x_across(hist_p, 2, 1, histR[1])
    x_across(hist_p, 1, 0, histL[0])
    x_across(sel_p, 2, 1, selR[1])
    x_across(sel_p, 1, 0, selL[0])
    aR[2].wait_recv()
    aR.append(z_send(gA, -3, zR, 0, half))
    aL[2].wait_recv()
    aL.append(z_send(gA, 3, zL, half, half))
    wr2.wait_recv()

    @pl.loop(0, 4)
    def _(d):
        small = wr_all[d].astype(F32)
        wide = [jnp.broadcast_to(small[h : h + 1, :], (32, 512)) for h in range(HEADS)]
        wide_v[d] = jnp.concatenate(wide, axis=0).T.astype(BF16)

    for copy in (*info, *load_own):
        copy.wait()
    for copy in (*on[0], *on[1], *on[2]):
        copy.wait_recv()
    for p in range(3):
        ranked(0, p)
    bR[2].wait_recv()
    bR.append(z_send(gB, -3, zR, 0, half))
    bL[2].wait_recv()
    bL.append(z_send(gB, 3, zL, half, half))
    for copy in (*ykR.values(), *ykL.values(), *yqR.values(), *yqL.values(), *aR, *aL):
        copy.wait_recv()

    @pl.loop(1, 3)
    def _(d):
        for p in range(3):
            ranked(d, p)

    x_across(hist_p, 3, 0, hist2R)
    x_across(hist_p, 3, 1, hist2L)
    x_across(sel_p, 3, 0, sel2R)
    x_across(sel_p, 3, 1, sel2L)
    for copy in used:
        copy.wait_recv()
    for p in range(3):
        ranked(3, p)

    @pl.loop(0, 4)
    def _(d):
        ranked(d, 3)

    back = []
    slot_of = {1: 1, 2: 3, 3: 2}
    for k in (1, 2, 3):
        s = slot_of[k]
        back.append(send(acc_v.at[s, 0], t_v.at[2 * s], xs[k - 1]))
        back.append(send(acc_v.at[s, 1], t_v.at[2 * s + 1], diag[k - 1]))
    back.append(send(acc_v.at[0, 1], t_v.at[1], other))
    t_v[0] = acc_v[0, 0]
    for copy in back:
        copy.wait_recv()
    teacher = t_v[0]
    for k in range(1, 8):
        teacher = teacher + t_v[k]
    live = lax.broadcasted_iota(jnp.int32, (8, 128), 1) < 32
    risen = jnp.where(live, jnp.exp(teacher / 6.0), 0.0)
    t_v[0] = risen / jnp.sum(risen, axis=1, keepdims=True)

    for r in range(4):
        rows = pl.ds(128 * r, 128)
        spots = lax.broadcasted_iota(jnp.int32, (128, 32), 0) == kept_ref[pl.ds(r, 1), :]
        aim = jnp.sum(jnp.where(spots, t_v[0, pl.ds(r, 1), pl.ds(0, 32)], 0.0), axis=1, keepdims=True)
        grad = st_v[rows, pl.ds(0, 1)] - aim
        for q in range(4):
            cols = pl.ds(256 * q, 256)
            hidden = hid_v[rows, cols]
            hg_v[rows, cols] = jnp.where(hidden > 0.0, grad * v_ref[:, cols].astype(F32), 0.0).astype(BF16)
            sum_v[pl.ds(8 * r, 8), cols] = jnp.sum((grad * hidden).reshape(16, 8, 256), axis=0)
    row = jnp.sum(sum_v[...], axis=0, keepdims=True)
    for k in range(8):
        s0_v[0, pl.ds(k, 1), :] = row[:, 128 * k : 128 * k + 128]
    sa = send(s0_v.at[0], s0_v.at[1], other)

    core = []

    def rows_of(k, side):
        return jnp.concatenate(
            [xt_v[pl.ds(pl.multiple_of(64 * (4 * k + j) + 32 * side, 32), 32), :] for j in range(4)], axis=0
        )

    for k in range(4):
        ga_s[pl.ds(4 * k, 4)] = dot(rows_of(k, 1 - c), hg_v[...]).astype(BF16).reshape(4, 32, 1024)
        core.append(send(ga_s.at[pl.ds(4 * k, 4)], ga_r.at[pl.ds(4 * k, 4)], other))
    for k in range(4):
        own_v[pl.ds(4 * k, 4)] = dot(rows_of(k, c), hg_v[...]).reshape(4, 32, 1024)
    for k in range(4):
        core[k].wait_recv()
        blocks = pl.ds(4 * k, 4)
        own_v[blocks] = own_v[blocks] + ga_r[blocks].astype(F32)
    sa.wait_recv()
    sx_v[x] = s0_v[0] + s0_v[1]

    n1, n2 = pl.ds(0, 512), pl.ds(512, 512)

    def along_x(side, h):
        return own_v[pl.ds(4 * side[GX] + 2 * h, 2), :, n1]

    def along_y(side, h):
        return jnp.stack([own_v[4 * (2 * h + j) + side[GY], :, n2] for j in range(2)])

    ways = ((along_x, xs, b1_s, b1_r), (along_y, ys, b2_s, b2_r))
    relay, direct = [], []
    for part, sides, out, into in ways:
        for h, device in ((0, sides[0]), (1, sides[2])):
            out[0, pl.ds(2 * h, 2)] = part(sides[1], h).astype(BF16)
            relay.append(send(out.at[0, pl.ds(2 * h, 2)], into.at[0, pl.ds(2 * h, 2)], device))
    sb = [send(sx_v.at[x], sx_v.at[x], xs[k]) for k in range(3)]
    for part, sides, out, into in ways:
        for h, device in ((1, sides[0]), (0, sides[2])):
            k = 2 - h
            out[k, pl.ds(2 * h, 2)] = part(device, h).astype(BF16)
            direct.append(send(out.at[k, pl.ds(2 * h, 2)], into.at[k, pl.ds(2 * h, 2)], device))
    for n, (part, sides, out, into) in enumerate(ways):
        for h, device in ((0, sides[0]), (1, sides[2])):
            relay[2 * n + h].wait_recv()
            k = 1 + h
            rows = pl.ds(2 * h, 2)
            out[k, rows] = (part(device, h) + into[0, rows].astype(F32)).astype(BF16)
            direct.append(send(out.at[k, rows], into.at[k, rows], device))
    for copy in sb:
        copy.wait_recv()
    sy_v[y] = (sx_v[0] + sx_v[1]) + (sx_v[2] + sx_v[3])
    sc = [send(sy_v.at[y], sy_v.at[y], ys[k]) for k in range(3)]
    for copy in direct:
        copy.wait_recv()
    a1_v[...] = own_v[pl.ds(4 * x, 4), :, n1] + (b1_r[1].astype(F32) + b1_r[2].astype(F32))
    for j in range(4):
        a2_v[j] = own_v[4 * j + y, :, n2] + (b2_r[1, j].astype(F32) + b2_r[2, j].astype(F32))
    third = []
    for k in (2, 1, 3):
        c1_s[k - 1] = a1_v[ys[k - 1][GY]].astype(BF16)
        third.append(send(c1_s.at[k - 1], c1_r.at[k - 1], ys[k - 1]))
    for k in (2, 1, 3):
        c2_s[k - 1] = a2_v[xs[k - 1][GX]].astype(BF16)
        third.append(send(c2_s.at[k - 1], c2_r.at[k - 1], xs[k - 1]))
    for copy in sc:
        copy.wait_recv()
    sz_v[z] = (sy_v[0] + sy_v[1]) + (sy_v[2] + sy_v[3])
    sd = [send(sz_v.at[z], sz_v.at[z], zs[k]) for k in range(NZ - 1)]
    for copy in third:
        copy.wait_recv()
    fin1 = a1_v[y] + (c1_r[0].astype(F32) + c1_r[1].astype(F32) + c1_r[2].astype(F32))
    fin2 = a2_v[x] + (c2_r[0].astype(F32) + c2_r[1].astype(F32) + c2_r[2].astype(F32))
    for k in range(4):
        fin_v[k] = fin1[:, 128 * k : 128 * k + 128]
        fin_v[4 + k] = fin2[:, 128 * k : 128 * k + 128]
    d_s[...] = fin_v[...].astype(BF16)

    fourth = []
    for k in (4, 3, 5, 2, 6, 1, 7):
        fourth.append(send(d_s.at[zs[k - 1][GZ]], d_r.at[k - 1], zs[k - 1]))
    for copy in fourth:
        copy.wait_recv()
    whole = fin_v[z]
    for k in range(NZ - 1):
        whole = whole + d_r[k].astype(F32)
    e_v[z] = whole
    fifth = [send(e_v.at[z], e_v.at[z], zs[k - 1]) for k in (4, 3, 5, 2, 6, 1, 7)]
    for copy in sd:
        copy.wait_recv()
    gs = sz_v[0]
    for k in range(1, NZ):
        gs = gs + sz_v[k]
    gs_ref[...] = gs
    for copy in fifth:
        copy.wait_recv()
    for k in range(NZ):
        gh_ref[:, pl.ds(128 * k, 128)] = e_v[k]
    for copy in used:
        copy.wait_send()


def vmem(*items):
    return [pltpu.VMEM(s, t) for s, t in items]


def body(
    offer_attribute_matrix,
    kept_offers,
    expert_target,
    sequence_extent,
    behaviour_sequence,
    inner_projection_matrix,
    student_rating_vector,
    asking_matrix,
    lookup_matrix,
    content_matrix,
    expert_rating_vector,
):
    v_row = student_rating_vector.reshape(1, 1024)
    grad_hidden, grad_score = pl.pallas_call(
        whole_kernel,
        out_shape=[jax.ShapeDtypeStruct((32, 1024), F32), jax.ShapeDtypeStruct((8, 128), F32)],
        in_specs=[pl.BlockSpec(memory_space=pl.ANY)] * 11,
        out_specs=[pl.BlockSpec(memory_space=pltpu.VMEM)] * 2,
        scratch_shapes=[
            *vmem(*[((2, 4, 32, 1024), BF16)] * 4, *[((2, 4, 128, 512), BF16)] * 4),
            pltpu.VMEM((4, 2, 8, 128), jnp.int32),
            pltpu.SMEM((64, 128), jnp.int32),
            *vmem(
                ((4, 1024, 512), BF16),
                ((4, 512, 512), BF16),
                ((4, 16, 512), BF16),
                ((4, 512, 256), BF16),
                ((4, 2, 8, 128), F32),
                ((4, 32), jnp.int32),
                ((4, 6), jnp.int32),
                ((1, 4), jnp.int32),
                ((1, 1024), BF16),
                ((1, 512), BF16),
                ((4, 128, 1024), BF16),
                ((1024, 1024), BF16),
                ((512, 512), BF16),
                ((512, 1024), F32),
                ((512, 128), F32),
                ((1024, 512), BF16),
                ((32, 1024), F32),
                ((512, 1024), BF16),
                ((8, 8, 128), F32),
                ((16, 32, 1024), BF16),
                ((16, 32, 1024), BF16),
                ((16, 32, 1024), F32),
                *[((3, 4, 32, 512), BF16)] * 4,
                *[((4, 32, 512), F32)] * 2,
                *[((3, 32, 512), BF16)] * 4,
                ((8, 32, 128), F32),
                ((8, 32, 128), BF16),
                ((7, 32, 128), BF16),
                ((8, 32, 128), F32),
                ((2, 8, 128), F32),
                ((4, 8, 128), F32),
                ((4, 8, 128), F32),
                ((8, 8, 128), F32),
            ),
            pltpu.SemaphoreType.DMA((160,)),
            pltpu.SemaphoreType.DMA((160,)),
            pltpu.SemaphoreType.DMA((24,)),
        ],
        compiler_params=pltpu.CompilerParams(
            collective_id=0, has_side_effects=True, vmem_limit_bytes=63 * 2**20
        ),
        name="distillation_backward",
    )(
        offer_attribute_matrix, kept_offers, expert_target, sequence_extent.reshape(1, 4),
        inner_projection_matrix, v_row, behaviour_sequence,
        asking_matrix[0], lookup_matrix[0], content_matrix[0], expert_rating_vector,
    )
    return grad_hidden, grad_score.reshape(1024)


def solution(mesh):
    torus = Mesh(mesh.devices.reshape(mesh.shape["group"], NX, NY, 2), GROUP_SHARD)
    return jax.shard_map(
        body,
        mesh=torus,
        in_specs=(
            P(GROUP_SHARD, None, None),
            P(GROUP_SHARD, None),
            P(GROUP_SHARD, None),
            P(GROUP_SHARD),
            P(GROUP_SHARD, None, None),
            P(),
            P(),
            P(SHARD, None, None),
            P(SHARD, None, None),
            P(SHARD, None, None),
            P(SHARD, None),
        ),
        out_specs=(P(SHARD, None), P()),
        check_vma=False,
    )
```

time: 465 us -> 93.8 us (0.20)
  waiting for transfers between devices: 141 us -> 0 us
  blocking collectives: 113 us -> 0 us
  Pallas kernels: 0 us -> 88.9 us
  matrix products: 68.6 us -> 0 us
  local copies, waits for them, and re-layouts: 71.1 us -> 4.12 us
  starting transfers between devices: 58.1 us -> 0 us
  other arithmetic: 8.46 us -> 0 us
    all_to_all x5 -> x0, waiting for transfers between devices: 141 us -> none  [the longest x1 102 us: body(): lax.all_to_all(send_hist, SHARD, split_axis=0, concat_axis=0, tiled=True)]
    pallas_call x0 -> x1, Pallas kernels: none -> 88.9 us  [body(): pl.pallas_call(whole_kernel, out_shape=[jax.ShapeDtypeStruct((32, 1024),...]
    dot_general x27 -> x0, matrix products: 68.6 us -> none  [the longest x4 23.8 us: ranker_block(): jnp.einsum('skhd,sjhd->shkj', queries, key_rows, preferred_element_type=j...]
    all_to_all x5 -> x0, starting transfers between devices: 58.1 us -> none  [the longest x1 25.2 us: turned_blocks(): result = lax.all_to_all(result, axes[k], k, k, tiled=True)]
    all_to_all x2 -> x0, blocking collectives: 56.8 us -> none  [the longest x1 53.1 us: sum_at_owner(): lax.all_to_all(blocks, axis, split_axis=0, concat_axis=0, tiled=True)]
    psum x4 -> x0, blocking collectives: 56.5 us -> none  [one_axis_at_a_time(): return functools.reduce(lax.psum, axes, value)]
    reshape x13 -> x1, local copies, waits for them, and re-layouts: 31.7 us -> 1.28 us  [body(): v_row = student_rating_vector.reshape(1, 1024)]
    convert_element_type x6 -> x0, local copies, waits for them, and re-layouts: 15.9 us -> none  [the longest x1 11.3 us: body(): send_hist = jnp.einsum('rts,rjf->sjf', placing_b, behaviour_sequence, pre...]
  transfers between devices with their start and end apart: 5 -> 0, of which waited for: 3 -> 0; matrix products, arithmetic and copies ran while one was open for 6% -> 0% of each run, Pallas kernels for 0% -> 0%
where the time goes in v2:
time: 93.8 us; the launch traced here: 93.6 us
  Pallas kernels  88.9 us (95%)
  local copies, waits for them, and re-layouts  4.12 us (4%)
    pallas_call x1, Pallas kernels, body(): pl.pallas_call(whole_kernel, out_shape=[jax.ShapeDtypeStruct((32, 1024),...  88.9 us
    unnamed x2, local copies, waits for them, and re-layouts  2.85 us

profile of v2, /device:TPU:2, one launch (start us, length us, event | category | flops | bytes accessed | tf_op | source)
XLA Modules:
  0.0 93.6 jit_solution(7738258851693985739)
XLA Ops:
  0.6 1.3 %reshape.14.v_in = bf16[1,1024]{1,0:T(2,128)(2,1)} reshape(bf16[1024]{0:T(1024)(128)(2,1)} %param.17) | data formatting | bytes 4096 | tf_op jit(solution)/shard_map/reshape | solution.py:495
  1.9 88.9 %distillation_backward.1 = (f32[32,1024]{1,0:T(8,128)}, f32[8,128]{1,0:T(8,128)}) custom-call(bf16[4,128,1024]{2,1,0:T(8,128)(2,1)} %x_ref.1, s32[4,32]{1,0:T(4,128)} %kept_in.1, s32[4,6]{1,0:T(4,128)} %target_in.1, s32[1,4]{1,0:T(1,128)} %bitcast.9, bf16[1024,1024]{1,0:T(8,128)(2,1)} %w1_ref.1, bf16[1,1024]{1,0:T(2,128)(2,1)} %reshape.14.v_in, ...), custom_call_target="tpu_custom_call" | custom-call | tf_op jit(solution)/shard_map/distillation_backward/pallas_call | solution.py:496
  90.8 1.6 %copy.15 = f32[32,1024]{1,0:T(8,128)} copy(f32[32,1024]{1,0:T(8,128)} %get-tuple-element.8) | data formatting | bytes 262144
  92.4 1.3 %copy.16 = f32[1024]{0:T(1024)} copy(f32[1024]{0:T(1024)} %bitcast.8) | data formatting | bytes 8192

commit v3 on v2

--- a/solution.py
+++ b/solution.py
@@ -16,7 +16,7 @@
 SHARD = (GX, GY, GC)
 GROUP_SHARD = (GZ, GX, GY, GC)
 NX, NY, NZ = 4, 4, 8
-SLICE = 96
+SLICE = 80
 SPLIT = SLICE * NZ
 NT = (((1,), (1,)), ((), ()))
 TN = (((0,), (0,)), ((), ()))
@@ -105,7 +105,8 @@
         plane = lax.rem(z + (step % NZ), NZ)
         return pl.ds(pl.multiple_of(plane * SLICE + start, 16), size)
 
-    half = SLICE // 2
+    half = SLICE // 32 * 16
+    more = SLICE - half
     tail = (1024 - SPLIT) // 2
     xR, xL, yR, yL, zR, zL = xs[0], xs[2], ys[0], ys[2], zs[0], zs[6]
 
@@ -139,6 +140,7 @@
     meta_all[0, 0, pl.ds(4, 1), pl.ds(0, 4)] = extent_ref[...]
     metaR = send(meta_all.at[0, 0], meta_all.at[2, 0], xR)
     metaL = send(meta_all.at[0, 0], meta_all.at[1, 0], xL)
+    meta2 = send(meta_all.at[0, 0], meta_all.at[3, 0], xs[1])
     meta_on = [send(meta_all.at[0, 0], meta_all.at[0, 1], other)]
 
     load_x.wait()
@@ -156,6 +158,7 @@
     wr_all[0] = dot(rating, wv_v[...], NT).astype(BF16)
     wrR = send(wr_all.at[0], wr_all.at[2], yR)
     wrL = send(wr_all.at[0], wr_all.at[1], yL)
+    wr2 = send(wr_all.at[0], wr_all.at[3], ys[1])
 
     zsR.wait_recv()
     zsL.wait_recv()
@@ -167,7 +170,7 @@
 
     aR, aL = [z_send(gA, 0, zR)], [z_send(gA, 0, zL)]
     zs2R = send(wq_all.at[2, zrows(0, 0, half)], wq_all.at[3, zrows(0, 0, half)], yR)
-    zs2L = send(wq_all.at[1, zrows(0, half, half)], wq_all.at[3, zrows(0, half, half)], yL)
+    zs2L = send(wq_all.at[1, zrows(0, half, more)], wq_all.at[3, zrows(0, half, more)], yL)
     yqR, yqL = {0: y_q(0, yR, 2)}, {1: y_q(1, yL, 1)}
     histR[1], histL[0] = x_hist(1, xR, 2), x_hist(0, xL, 1)
     selR[1], selL[0] = x_sel(1, xR, 2), x_sel(0, xL, 1)
@@ -213,7 +216,6 @@
 
     metaR.wait_recv()
     metaL.wait_recv()
-    meta2 = send(meta_all.at[2, 0], meta_all.at[3, 0], xR)
     meta_on.append(send(meta_all.at[2, 0], meta_all.at[2, 1], other))
     meta_on.append(send(meta_all.at[1, 0], meta_all.at[1, 1], other))
     zs2R.wait_recv()
@@ -229,9 +231,6 @@
     tower(2)
     sel2R = x_forward(sel_p, 0, selR[0])
     sel2L = x_forward(sel_p, 1, selL[1])
-    wrR.wait_recv()
-    wrL.wait_recv()
-    wr2 = send(wr_all.at[2], wr_all.at[3], yR)
     meta2.wait_recv()
     meta_on.append(send(meta_all.at[3, 0], meta_all.at[3, 1], other))
     bR[0].wait_recv()
@@ -241,14 +240,6 @@
     tower(3)
     y_forward(0, ykR[0], yqR[0])
     y_forward(1, ykL[1], yqL[1])
-    aR[1].wait_recv()
-    aR.append(z_send(gA, -2, zR))
-    aL[1].wait_recv()
-    aL.append(z_send(gA, 2, zL))
-    bR[1].wait_recv()
-    bR.append(z_send(gB, -2, zR))
-    bL[1].wait_recv()
-    bL.append(z_send(gB, 2, zL))
     for copy in meta_on:
         copy.wait_recv()
     info = [
@@ -297,52 +288,66 @@
             mark = out_row == jnp.where(found == 1, i, -1)
             acc_v[p, core] = acc_v[p, core] + jnp.where(mark, score, 0.0)
 
+    def widened(d):
+        small = wr_all[d].astype(F32)
+        wide = [jnp.broadcast_to(small[h : h + 1, :], (32, 512)) for h in range(HEADS)]
+        wide_v[d] = jnp.concatenate(wide, axis=0).T.astype(BF16)
+
+    def expert_run(low, high, groups):
+        @pl.loop(low, high)
+        def _(d):
+            for p in groups:
+                ranked(d, p)
+
+    def arrived(*copies):
+        for copy in copies:
+            copy.wait_recv()
+
+    for copy in (*info, *load_own):
+        copy.wait()
+    widened(0)
+    arrived(*on[0])
+    ranked(0, 0)
+    aR[1].wait_recv()
+    aR.append(z_send(gA, -2, zR))
+    aL[1].wait_recv()
+    aL.append(z_send(gA, 2, zL))
+    bR[1].wait_recv()
+    bR.append(z_send(gB, -2, zR))
+    bL[1].wait_recv()
+    bL.append(z_send(gB, 2, zL))
     x_across(hist_p, 2, 1, histR[1])
     x_across(hist_p, 1, 0, histL[0])
     x_across(sel_p, 2, 1, selR[1])
     x_across(sel_p, 1, 0, selL[0])
+    arrived(wrR, wrL, wr2)
+
+    @pl.loop(1, 4)
+    def _(d):
+        widened(d)
+
     aR[2].wait_recv()
     aR.append(z_send(gA, -3, zR, 0, half))
     aL[2].wait_recv()
-    aL.append(z_send(gA, 3, zL, half, half))
-    wr2.wait_recv()
-
-    @pl.loop(0, 4)
-    def _(d):
-        small = wr_all[d].astype(F32)
-        wide = [jnp.broadcast_to(small[h : h + 1, :], (32, 512)) for h in range(HEADS)]
-        wide_v[d] = jnp.concatenate(wide, axis=0).T.astype(BF16)
-
-    for copy in (*info, *load_own):
-        copy.wait()
-    for copy in (*on[0], *on[1], *on[2]):
-        copy.wait_recv()
-    for p in range(3):
-        ranked(0, p)
+    aL.append(z_send(gA, 3, zL, half, more))
+    arrived(*on[1], *on[2])
+    ranked(0, 1)
+    ranked(0, 2)
     bR[2].wait_recv()
     bR.append(z_send(gB, -3, zR, 0, half))
     bL[2].wait_recv()
-    bL.append(z_send(gB, 3, zL, half, half))
-    for copy in (*ykR.values(), *ykL.values(), *yqR.values(), *yqL.values(), *aR, *aL):
-        copy.wait_recv()
-
-    @pl.loop(1, 3)
-    def _(d):
-        for p in range(3):
-            ranked(d, p)
-
+    bL.append(z_send(gB, 3, zL, half, more))
     x_across(hist_p, 3, 0, hist2R)
     x_across(hist_p, 3, 1, hist2L)
     x_across(sel_p, 3, 0, sel2R)
     x_across(sel_p, 3, 1, sel2L)
-    for copy in used:
-        copy.wait_recv()
-    for p in range(3):
-        ranked(3, p)
-
-    @pl.loop(0, 4)
-    def _(d):
-        ranked(d, 3)
+    arrived(*ykR.values(), *ykL.values(), *yqR.values(), *yqL.values(), *aR, *aL)
+    arrived(*on[1], *on[2])
+    expert_run(1, 3, range(3))
+    arrived(*on[3])
+    expert_run(0, 3, (3,))
+    arrived(*used)
+    expert_run(3, 4, range(4))
 
     back = []
     slot_of = {1: 1, 2: 3, 3: 2}

time: 93.8 us -> 88.5 us (0.943)
  Pallas kernels: 88.9 us -> 83.5 us
    pallas_call x1, Pallas kernels: 88.9 us -> 83.5 us  [body(): pl.pallas_call(whole_kernel, out_shape=[jax.ShapeDtypeStruct((32, 1024),...]
where the time goes in v3:
time: 88.5 us; the launch traced here: 88.2 us
  Pallas kernels  83.5 us (94%)
  local copies, waits for them, and re-layouts  4.12 us (5%)
    pallas_call x1, Pallas kernels, body(): pl.pallas_call(whole_kernel, out_shape=[jax.ShapeDtypeStruct((32, 1024),...  83.5 us
    unnamed x2, local copies, waits for them, and re-layouts  2.85 us

profile of v3, /device:TPU:2, one launch (start us, length us, event | category | flops | bytes accessed | tf_op | source)
XLA Modules:
  0.0 88.2 jit_solution(4663276601646068186)
XLA Ops:
  0.6 1.3 %reshape.14.v_in = bf16[1,1024]{1,0:T(2,128)(2,1)} reshape(bf16[1024]{0:T(1024)(128)(2,1)} %param.17) | data formatting | bytes 4096 | tf_op jit(solution)/shard_map/reshape | solution.py:500
  1.9 83.5 %distillation_backward.1 = (f32[32,1024]{1,0:T(8,128)}, f32[8,128]{1,0:T(8,128)}) custom-call(bf16[4,128,1024]{2,1,0:T(8,128)(2,1)} %x_ref.1, s32[4,32]{1,0:T(4,128)} %kept_in.1, s32[4,6]{1,0:T(4,128)} %target_in.1, s32[1,4]{1,0:T(1,128)} %bitcast.9, bf16[1024,1024]{1,0:T(8,128)(2,1)} %w1_ref.1, bf16[1,1024]{1,0:T(2,128)(2,1)} %reshape.14.v_in, ...), custom_call_target="tpu_custom_call" | custom-call | tf_op jit(solution)/shard_map/distillation_backward/pallas_call | solution.py:501
  85.4 1.6 %copy.15 = f32[32,1024]{1,0:T(8,128)} copy(f32[32,1024]{1,0:T(8,128)} %get-tuple-element.8) | data formatting | bytes 262144
  86.9 1.3 %copy.16 = f32[1024]{0:T(1024)} copy(f32[1024]{0:T(1024)} %bitcast.8) | data formatting | bytes 8192

commit v4 on v3

--- a/solution.py
+++ b/solution.py
@@ -16,7 +16,7 @@
 SHARD = (GX, GY, GC)
 GROUP_SHARD = (GZ, GX, GY, GC)
 NX, NY, NZ = 4, 4, 8
-SLICE = 80
+SLICE = 64
 SPLIT = SLICE * NZ
 NT = (((1,), (1,)), ((), ()))
 TN = (((0,), (0,)), ((), ()))
@@ -49,7 +49,7 @@
     gh_ref, gs_ref,
     sel0, sel1, sel2, sel3, hist0, hist1, hist2, hist3,
     meta_all, meta_s, wq_all, wk_all, wr_all, wide_v, acc_v,
-    kept_ref, target_ref, extent_ref, v_ref, rat_ref,
+    kept_ref, target_ref, extent_ref, v_rows, v_ref, rat_ref,
     x_v, w1_v, wv_v, hid_v, st_v, xt_v, sum_v,
     hg_v, t_v, ga_s, ga_r, own_v, b1_s, b1_r, b2_s, b2_r, a1_v, a2_v,
     c1_s, c1_r, c2_s, c2_r, fin_v, d_s, d_r, e_v, s0_v, sx_v, sy_v, sz_v, send_sem, recv_sem, load_sem,
@@ -83,7 +83,7 @@
         load(src, dst)
         for src, dst in (
             (target_in, target_ref), (extent_in, extent_ref), (kept_in, kept_ref), (rat_in, rat_ref),
-            (v_in, v_ref),
+            (v_in, v_rows),
         )
     ]
     load_x = load(x_ref, x_v)
@@ -143,6 +143,9 @@
     meta2 = send(meta_all.at[0, 0], meta_all.at[3, 0], xs[1])
     meta_on = [send(meta_all.at[0, 0], meta_all.at[0, 1], other)]
 
+    for k in range(8):
+        v_ref[:, pl.ds(128 * k, 128)] = v_rows[...].astype(F32)[k : k + 1, :]
+
     load_x.wait()
     for r in range(4):
         onehot = (
@@ -186,7 +189,7 @@
             cols = pl.ds(256 * q, 256)
             hidden = jnp.maximum(dot(block, w1_v[:, cols]), 0.0)
             hid_v[rows, cols] = hidden
-            scores = scores + jnp.sum(hidden * v_ref[:, cols].astype(F32), axis=1, keepdims=True)
+            scores = scores + jnp.sum(hidden * v_ref[:, cols], axis=1, keepdims=True)
         weights = jnp.exp(scores)
         st_v[rows, :] = jnp.broadcast_to(weights / jnp.sum(weights, axis=0, keepdims=True), (128, 128))
         xt_v[:, rows] = block.T
@@ -221,25 +224,21 @@
     zs2R.wait_recv()
     zs2L.wait_recv()
     bR, bL = [z_send(gB, 0, zR)], [z_send(gB, 0, zL)]
-    tower(1)
-    hist2R = x_forward(hist_p, 0, histR[0])
-    hist2L = x_forward(hist_p, 1, histL[1])
-    aR[0].wait_recv()
-    aR.append(z_send(gA, -1, zR))
-    aL[0].wait_recv()
-    aL.append(z_send(gA, 1, zL))
-    tower(2)
-    sel2R = x_forward(sel_p, 0, selR[0])
-    sel2L = x_forward(sel_p, 1, selL[1])
     meta2.wait_recv()
     meta_on.append(send(meta_all.at[3, 0], meta_all.at[3, 1], other))
-    bR[0].wait_recv()
-    bR.append(z_send(gB, -1, zR))
-    bL[0].wait_recv()
-    bL.append(z_send(gB, 1, zL))
+
+    def z_step(group, rights, lefts, k):
+        cut = k == 3
+        rights[k - 1].wait_recv()
+        rights.append(z_send(group, -k, zR, 0, half if cut else SLICE))
+        lefts[k - 1].wait_recv()
+        lefts.append(z_send(group, k, zL, half if cut else 0, more if cut else SLICE))
+
+    tower(1)
+    z_step(gA, aR, aL, 1)
+    tower(2)
+    z_step(gB, bR, bL, 1)
     tower(3)
-    y_forward(0, ykR[0], yqR[0])
-    y_forward(1, ykL[1], yqL[1])
     for copy in meta_on:
         copy.wait_recv()
     info = [
@@ -308,54 +307,44 @@
     widened(0)
     arrived(*on[0])
     ranked(0, 0)
-    aR[1].wait_recv()
-    aR.append(z_send(gA, -2, zR))
-    aL[1].wait_recv()
-    aL.append(z_send(gA, 2, zL))
-    bR[1].wait_recv()
-    bR.append(z_send(gB, -2, zR))
-    bL[1].wait_recv()
-    bL.append(z_send(gB, 2, zL))
+    z_step(gA, aR, aL, 2)
+    arrived(wrR, wrL, wr2)
+
+    @pl.loop(1, 4)
+    def _(d):
+        widened(d)
+
+    z_step(gB, bR, bL, 2)
+    hist2R = x_forward(hist_p, 0, histR[0])
+    hist2L = x_forward(hist_p, 1, histL[1])
+    sel2R = x_forward(sel_p, 0, selR[0])
+    sel2L = x_forward(sel_p, 1, selL[1])
+    y_forward(0, ykR[0], yqR[0])
+    y_forward(1, ykL[1], yqL[1])
+    z_step(gA, aR, aL, 3)
     x_across(hist_p, 2, 1, histR[1])
     x_across(hist_p, 1, 0, histL[0])
     x_across(sel_p, 2, 1, selR[1])
     x_across(sel_p, 1, 0, selL[0])
-    arrived(wrR, wrL, wr2)
-
-    @pl.loop(1, 4)
-    def _(d):
-        widened(d)
-
-    aR[2].wait_recv()
-    aR.append(z_send(gA, -3, zR, 0, half))
-    aL[2].wait_recv()
-    aL.append(z_send(gA, 3, zL, half, more))
     arrived(*on[1], *on[2])
     ranked(0, 1)
     ranked(0, 2)
-    bR[2].wait_recv()
-    bR.append(z_send(gB, -3, zR, 0, half))
-    bL[2].wait_recv()
-    bL.append(z_send(gB, 3, zL, half, more))
+    z_step(gB, bR, bL, 3)
     x_across(hist_p, 3, 0, hist2R)
     x_across(hist_p, 3, 1, hist2L)
     x_across(sel_p, 3, 0, sel2R)
     x_across(sel_p, 3, 1, sel2L)
     arrived(*ykR.values(), *ykL.values(), *yqR.values(), *yqL.values(), *aR, *aL)
-    arrived(*on[1], *on[2])
     expert_run(1, 3, range(3))
     arrived(*on[3])
     expert_run(0, 3, (3,))
     arrived(*used)
-    expert_run(3, 4, range(4))
-
     back = []
-    slot_of = {1: 1, 2: 3, 3: 2}
-    for k in (1, 2, 3):
-        s = slot_of[k]
-        back.append(send(acc_v.at[s, 0], t_v.at[2 * s], xs[k - 1]))
-        back.append(send(acc_v.at[s, 1], t_v.at[2 * s + 1], diag[k - 1]))
-    back.append(send(acc_v.at[0, 1], t_v.at[1], other))
+    for p, k in ((3, 2), (1, 1), (2, 3), (0, 0)):
+        ranked(3, p)
+        if k:
+            back.append(send(acc_v.at[p, 0], t_v.at[2 * p], xs[k - 1]))
+        back.append(send(acc_v.at[p, 1], t_v.at[2 * p + 1], diag[k - 1] if k else other))
     t_v[0] = acc_v[0, 0]
     for copy in back:
         copy.wait_recv()
@@ -374,7 +363,7 @@
         for q in range(4):
             cols = pl.ds(256 * q, 256)
             hidden = hid_v[rows, cols]
-            hg_v[rows, cols] = jnp.where(hidden > 0.0, grad * v_ref[:, cols].astype(F32), 0.0).astype(BF16)
+            hg_v[rows, cols] = jnp.where(hidden > 0.0, grad * v_ref[:, cols], 0.0).astype(BF16)
             sum_v[pl.ds(8 * r, 8), cols] = jnp.sum((grad * hidden).reshape(16, 8, 256), axis=0)
     row = jnp.sum(sum_v[...], axis=0, keepdims=True)
     for k in range(8):
@@ -388,18 +377,6 @@
             [xt_v[pl.ds(pl.multiple_of(64 * (4 * k + j) + 32 * side, 32), 32), :] for j in range(4)], axis=0
         )
 
-    for k in range(4):
-        ga_s[pl.ds(4 * k, 4)] = dot(rows_of(k, 1 - c), hg_v[...]).astype(BF16).reshape(4, 32, 1024)
-        core.append(send(ga_s.at[pl.ds(4 * k, 4)], ga_r.at[pl.ds(4 * k, 4)], other))
-    for k in range(4):
-        own_v[pl.ds(4 * k, 4)] = dot(rows_of(k, c), hg_v[...]).reshape(4, 32, 1024)
-    for k in range(4):
-        core[k].wait_recv()
-        blocks = pl.ds(4 * k, 4)
-        own_v[blocks] = own_v[blocks] + ga_r[blocks].astype(F32)
-    sa.wait_recv()
-    sx_v[x] = s0_v[0] + s0_v[1]
-
     n1, n2 = pl.ds(0, 512), pl.ds(512, 512)
 
     def along_x(side, h):
@@ -410,16 +387,38 @@
 
     ways = ((along_x, xs, b1_s, b1_r), (along_y, ys, b2_s, b2_r))
     relay, direct = [], []
-    for part, sides, out, into in ways:
+
+    def to_relay(part, sides, out, into):
         for h, device in ((0, sides[0]), (1, sides[2])):
             out[0, pl.ds(2 * h, 2)] = part(sides[1], h).astype(BF16)
             relay.append(send(out.at[0, pl.ds(2 * h, 2)], into.at[0, pl.ds(2 * h, 2)], device))
+
+    def to_next(part, sides, out, into, h):
+        k, device = 2 - h, sides[0] if h == 1 else sides[2]
+        out[k, pl.ds(2 * h, 2)] = part(device, h).astype(BF16)
+        direct.append(send(out.at[k, pl.ds(2 * h, 2)], into.at[k, pl.ds(2 * h, 2)], device))
+
+    order = [xs[1][GX], xs[0][GX], xs[2][GX], x]
+    for k in range(4):
+        blocks = pl.ds(4 * order[k], 4)
+        ga_s[blocks] = dot(rows_of(order[k], 1 - c), hg_v[...]).astype(BF16).reshape(4, 32, 1024)
+        core.append(send(ga_s.at[blocks], ga_r.at[blocks], other))
+    for k in range(4):
+        own_v[pl.ds(4 * order[k], 4)] = dot(rows_of(order[k], c), hg_v[...]).reshape(4, 32, 1024)
+    for k in range(4):
+        core[k].wait_recv()
+        blocks = pl.ds(4 * order[k], 4)
+        own_v[blocks] = own_v[blocks] + ga_r[blocks].astype(F32)
+        if k == 0:
+            to_relay(*ways[0])
+        if k in (1, 2):
+            to_next(*ways[0], 2 - k)
+    to_relay(*ways[1])
+    to_next(*ways[1], 1)
+    to_next(*ways[1], 0)
+    sa.wait_recv()
+    sx_v[x] = s0_v[0] + s0_v[1]
     sb = [send(sx_v.at[x], sx_v.at[x], xs[k]) for k in range(3)]
-    for part, sides, out, into in ways:
-        for h, device in ((1, sides[0]), (0, sides[2])):
-            k = 2 - h
-            out[k, pl.ds(2 * h, 2)] = part(device, h).astype(BF16)
-            direct.append(send(out.at[k, pl.ds(2 * h, 2)], into.at[k, pl.ds(2 * h, 2)], device))
     for n, (part, sides, out, into) in enumerate(ways):
         for h, device in ((0, sides[0]), (1, sides[2])):
             relay[2 * n + h].wait_recv()
@@ -497,7 +496,7 @@
     content_matrix,
     expert_rating_vector,
 ):
-    v_row = student_rating_vector.reshape(1, 1024)
+    v_row = student_rating_vector.reshape(8, 128)
     grad_hidden, grad_score = pl.pallas_call(
         whole_kernel,
         out_shape=[jax.ShapeDtypeStruct((32, 1024), F32), jax.ShapeDtypeStruct((8, 128), F32)],
@@ -516,7 +515,8 @@
                 ((4, 32), jnp.int32),
                 ((4, 6), jnp.int32),
                 ((1, 4), jnp.int32),
-                ((1, 1024), BF16),
+                ((8, 128), BF16),
+                ((1, 1024), F32),
                 ((1, 512), BF16),
                 ((4, 128, 1024), BF16),
                 ((1024, 1024), BF16),

time: 88.5 us -> 86.3 us (0.975)
  local copies, waits for them, and re-layouts: 4.12 us -> 2.85 us
    reshape x1 -> x0, local copies, waits for them, and re-layouts: 1.28 us -> none  [body(): v_row = student_rating_vector.reshape(1, 1024)]
where the time goes in v4:
time: 86.3 us; the launch traced here: 86.2 us
  Pallas kernels  82.7 us (96%)
  local copies, waits for them, and re-layouts  2.85 us (3%)
    pallas_call x1, Pallas kernels, body(): pl.pallas_call(whole_kernel, out_shape=[jax.ShapeDtypeStruct((32, 1024),...  82.7 us
    unnamed x2, local copies, waits for them, and re-layouts  2.85 us

profile of v4, /device:TPU:2, one launch (start us, length us, event | category | flops | bytes accessed | tf_op | source)
XLA Modules:
  0.0 86.2 jit_solution(8633095015875734548)
XLA Ops:
  0.6 82.7 %distillation_backward.1 = (f32[32,1024]{1,0:T(8,128)}, f32[8,128]{1,0:T(8,128)}) custom-call(bf16[4,128,1024]{2,1,0:T(8,128)(2,1)} %x_ref.1, s32[4,32]{1,0:T(4,128)} %kept_in.1, s32[4,6]{1,0:T(4,128)} %target_in.1, s32[1,4]{1,0:T(1,128)} %bitcast.11, bf16[1024,1024]{1,0:T(8,128)(2,1)} %w1_ref.1, bf16[8,128]{1,0:T(8,128)(2,1)} %bitcast.10, ...), custom_call_target="tpu_custom_call" | custom-call | tf_op jit(solution)/shard_map/distillation_backward/pallas_call | solution.py:500
  83.3 1.6 %copy.15 = f32[32,1024]{1,0:T(8,128)} copy(f32[32,1024]{1,0:T(8,128)} %get-tuple-element.8) | data formatting | bytes 262144
  84.9 1.3 %copy.16 = f32[1024]{0:T(1024)} copy(f32[1024]{0:T(1024)} %bitcast.9) | data formatting | bytes 8192

commit v5 on v4

--- a/solution.py
+++ b/solution.py
@@ -16,7 +16,7 @@
 SHARD = (GX, GY, GC)
 GROUP_SHARD = (GZ, GX, GY, GC)
 NX, NY, NZ = 4, 4, 8
-SLICE = 64
+SLICE = 80
 SPLIT = SLICE * NZ
 NT = (((1,), (1,)), ((), ()))
 TN = (((0,), (0,)), ((), ()))
@@ -79,6 +79,14 @@
         loads.append(copy)
         return copy
 
+    xs = [at(GX, k, NX) for k in (1, 2, 3)]
+    ys = [at(GY, k, NY) for k in (1, 2, 3)]
+    zs = [at(GZ, k, NZ) for k in range(1, NZ)]
+    diag = [{**d, **other} for d in xs]
+    peers = [*xs, *ys, *zs, *diag, other]
+    barrier = pltpu.get_barrier_semaphore()
+    for peer in peers:
+        pl.semaphore_signal(barrier, inc=1, device_id=peer, device_id_type=MESH)
     load_small = [
         load(src, dst)
         for src, dst in (
@@ -90,15 +98,6 @@
     load_wv = load(wv_ref, wv_v)
     load_own = [load(hist_ref, hist0.at[0]), load(wq_ref, wq_all.at[0]), load(wk_ref, wk_all.at[0])]
     load_w1 = load(w1_ref, w1_v)
-
-    xs = [at(GX, k, NX) for k in (1, 2, 3)]
-    ys = [at(GY, k, NY) for k in (1, 2, 3)]
-    zs = [at(GZ, k, NZ) for k in range(1, NZ)]
-    diag = [{**d, **other} for d in xs]
-    peers = [*xs, *ys, *zs, *diag, other]
-    barrier = pltpu.get_barrier_semaphore()
-    for peer in peers:
-        pl.semaphore_signal(barrier, inc=1, device_id=peer, device_id_type=MESH)
     pl.semaphore_wait(barrier, len(peers))
 
     def zrows(step, start=0, size=SLICE):
@@ -314,13 +313,13 @@
     def _(d):
         widened(d)
 
-    z_step(gB, bR, bL, 2)
     hist2R = x_forward(hist_p, 0, histR[0])
     hist2L = x_forward(hist_p, 1, histL[1])
     sel2R = x_forward(sel_p, 0, selR[0])
     sel2L = x_forward(sel_p, 1, selL[1])
     y_forward(0, ykR[0], yqR[0])
     y_forward(1, ykL[1], yqL[1])
+    z_step(gB, bR, bL, 2)
     z_step(gA, aR, aL, 3)
     x_across(hist_p, 2, 1, histR[1])
     x_across(hist_p, 1, 0, histL[0])

time: 86.3 us -> 86.1 us (level)
  no operation moved by 1% of the time
where the time goes in v5:
time: 86.1 us; the launch traced here: 86 us
  Pallas kernels  82.5 us (96%)
  local copies, waits for them, and re-layouts  2.85 us (3%)
    pallas_call x1, Pallas kernels, body(): pl.pallas_call(whole_kernel, out_shape=[jax.ShapeDtypeStruct((32, 1024),...  82.5 us
    unnamed x2, local copies, waits for them, and re-layouts  2.85 us

profile of v5, /device:TPU:2, one launch (start us, length us, event | category | flops | bytes accessed | tf_op | source)
XLA Modules:
  0.0 86.0 jit_solution(5432216363670697042)
XLA Ops:
  0.6 82.5 %distillation_backward.1 = (f32[32,1024]{1,0:T(8,128)}, f32[8,128]{1,0:T(8,128)}) custom-call(bf16[4,128,1024]{2,1,0:T(8,128)(2,1)} %x_ref.1, s32[4,32]{1,0:T(4,128)} %kept_in.1, s32[4,6]{1,0:T(4,128)} %target_in.1, s32[1,4]{1,0:T(1,128)} %bitcast.11, bf16[1024,1024]{1,0:T(8,128)(2,1)} %w1_ref.1, bf16[8,128]{1,0:T(8,128)(2,1)} %bitcast.10, ...), custom_call_target="tpu_custom_call" | custom-call | tf_op jit(solution)/shard_map/distillation_backward/pallas_call | solution.py:499
  83.2 1.6 %copy.15 = f32[32,1024]{1,0:T(8,128)} copy(f32[32,1024]{1,0:T(8,128)} %get-tuple-element.8) | data formatting | bytes 262144
  84.7 1.3 %copy.16 = f32[1024]{0:T(1024)} copy(f32[1024]{0:T(1024)} %bitcast.9) | data formatting | bytes 8192
